TPU v7x, 32 devices: a whole 2x2x4 slice. The times are simulated.
32 devices in a mesh: section: 2 (over core), dp: 16 (over z, y, x).
Axes of the slice: x: 2, y: 2, z: 4, core: 2. Of those that a mesh axis runs over, the one named last changes fastest.
Arguments:
- patches: bfloat16 [32, 24, 24, 1024], P('dp'), may hold values from -6 to 6
- grid_counts: int32 [16], P('dp'), may hold values from 1 to 2, as said below
- reduce_w: bfloat16 [2, 1024, 1024], P('section'), may hold values from -0.1875 to 0.1875
- conv_w: bfloat16 [2, 9, 1024, 1024], P('section'), may hold values from -0.0625 to 0.0625
- expand_w: bfloat16 [2, 1024, 1024], P('section'), may hold values from -0.1875 to 0.1875
- norm_gain: float32 [2, 3072], P('section'), may hold values from 0.25 to 1.75
- norm_bias: float32 [2, 3072], P('section'), may hold values from -1.8 to 1.8
- readout_w: bfloat16 [1024, 4096], replicated, may hold values from -0.1875 to 0.1875
- readout_b: float32 [4096], replicated, may hold values from -1.8 to 1.8
- out_grad: bfloat16 [32, 12, 12, 4096], P('dp'), may hold values from -6 to 6
Outputs:
- mixed: bfloat16 [32, 12, 12, 4096], P('dp', None, None, 'section')
- patch_grad: bfloat16 [32, 24, 24, 1024], P('dp', None, None, 'section')
- grad_reduce: float32 [2, 1024, 1024], P('section', 'dp')
- grad_conv: float32 [2, 9216, 1024], P('section', None, 'dp')
- grad_expand: float32 [2, 1024, 1024], P('section', None, 'dp')
- grad_norm: float32 [2, 6144], P('section', 'dp')
- grad_readout: float32 [1024, 4096], P(None, ('section', 'dp'))
- grad_readout_bias: float32 [4096], P(('section', 'dp'))
Inputs may be any that keep to these rules, and one draw needn't show every extreme that they name: `grid_counts`: the 1 images of one dp device have at most 2 grids together; in every draw some device has exactly 2.
All inputs are finite; a program needn't handle non-finite values.
Results may differ from a plain program's by a relative error of at most 0.018.
Values may be sent and summed in bfloat16 or wider, within the bound.
A program may use at most 576 MiB of HBM per device.

v0:
```python
import jax
import jax.numpy as jnp
from jax import lax
from jax.sharding import PartitionSpec as P

MICRO = 2


norm_epsilon = 1e-05


def from_behind(x, axis, by):
    size = lax.axis_size(axis)
    pairs = [(i, i + by) for i in range(size) if 0 <= i + by < size]
    return lax.ppermute(x, axis, pairs)


def norm_silu(values, scale_vec, shift_vec):
    average = jnp.mean(values, axis=-1, keepdims=True)
    centered = values - average
    variance = jnp.mean(centered * centered, axis=-1, keepdims=True)
    return jax.nn.silu(centered * lax.rsqrt(variance + norm_epsilon) * scale_vec + shift_vec)


def norm_pullback(values, scale_vec, shift_vec, grad_out):
    _, pullback = jax.vjp(norm_silu, values, scale_vec, shift_vec)
    return pullback(grad_out)


def conv_forward(activity, conv_weights):
    grid_side = activity.shape[1]
    padded = jnp.pad(activity, ((0, 0), (1, 1), (1, 1), (0, 0)))
    summed = None
    for tap_index in range(9):
        vertical = tap_index // 3
        lateral = tap_index % 3
        window = padded[:, vertical : vertical + grid_side, lateral : lateral + grid_side, :]
        partial_sum = jnp.einsum(
            "gijc,cd->gijd", window, conv_weights[tap_index], preferred_element_type=jnp.float32
        )
        summed = partial_sum if summed is None else summed + partial_sum
    return summed


def conv_backward(activity, conv_weights, grad_low):
    grid_side = activity.shape[1]
    padded = jnp.pad(activity, ((0, 0), (1, 1), (1, 1), (0, 0)))
    grad_padded = jnp.zeros(padded.shape, jnp.float32)
    tap_grads = []
    for tap_index in range(9):
        vertical = tap_index // 3
        lateral = tap_index % 3
        window = padded[:, vertical : vertical + grid_side, lateral : lateral + grid_side, :]
        tap_grads.append(
            jnp.einsum("gijc,gijd->cd", window, grad_low, preferred_element_type=jnp.float32)
        )
        spread_back = jnp.einsum(
            "gijd,cd->gijc", grad_low, conv_weights[tap_index], preferred_element_type=jnp.float32
        )
        grad_padded = grad_padded.at[
            :, vertical : vertical + grid_side, lateral : lateral + grid_side, :
        ].add(spread_back)
    return (grad_padded[:, 1:-1, 1:-1, :], jnp.stack(tap_grads))


def block_forward(inputs_low, weights, norm_gains, norm_biases):
    reduce_weights, conv_weights, expand_weights = weights
    middle = reduce_weights.shape[1]
    first_pre = jnp.einsum(
        "gijc,cd->gijd", inputs_low, reduce_weights, preferred_element_type=jnp.float32
    )
    first_act = norm_silu(first_pre, norm_gains[:middle], norm_biases[:middle]).astype(jnp.bfloat16)
    conv_pre = conv_forward(first_act, conv_weights)
    conv_act = norm_silu(
        conv_pre, norm_gains[middle : 2 * middle], norm_biases[middle : 2 * middle]
    ).astype(jnp.bfloat16)
    expand_pre = jnp.einsum(
        "gijc,cd->gijd", conv_act, expand_weights, preferred_element_type=jnp.float32
    )
    block_out = inputs_low.astype(jnp.float32) + norm_silu(
        expand_pre, norm_gains[2 * middle :], norm_biases[2 * middle :]
    )
    return (block_out, (first_pre, first_act, conv_pre, conv_act, expand_pre))


def block_backward(inputs_low, weights, norm_gains, norm_biases, saved, grad_out):
    reduce_weights, conv_weights, expand_weights = weights
    first_pre, first_act, conv_pre, conv_act, expand_pre = saved
    middle = reduce_weights.shape[1]
    grad_expand_pre, gain_last, bias_last = norm_pullback(
        expand_pre, norm_gains[2 * middle :], norm_biases[2 * middle :], grad_out
    )
    grad_expand_pre = grad_expand_pre.astype(jnp.bfloat16)
    expand_grad = jnp.einsum(
        "gijc,gijd->cd", conv_act, grad_expand_pre, preferred_element_type=jnp.float32
    )
    grad_conv_act = jnp.einsum(
        "gijd,cd->gijc", grad_expand_pre, expand_weights, preferred_element_type=jnp.float32
    )
    grad_conv_pre, gain_conv, bias_conv = norm_pullback(
        conv_pre, norm_gains[middle : 2 * middle], norm_biases[middle : 2 * middle], grad_conv_act
    )
    grad_conv_pre = grad_conv_pre.astype(jnp.bfloat16)
    grad_first_act, conv_grad = conv_backward(first_act, conv_weights, grad_conv_pre)
    grad_first_pre, gain_first, bias_first = norm_pullback(
        first_pre, norm_gains[:middle], norm_biases[:middle], grad_first_act
    )
    grad_first_pre = grad_first_pre.astype(jnp.bfloat16)
    reduce_grad = jnp.einsum(
        "gijc,gijd->cd", inputs_low, grad_first_pre, preferred_element_type=jnp.float32
    )
    grad_inputs = grad_out + jnp.einsum(
        "gijd,cd->gijc", grad_first_pre, reduce_weights, preferred_element_type=jnp.float32
    )
    norm_grads = jnp.concatenate(
        [gain_first, gain_conv, gain_last, bias_first, bias_conv, bias_last]
    )
    return (
        grad_inputs,
        (reduce_grad, conv_grad.reshape(9 * middle, middle), expand_grad, norm_grads),
    )


def pool_cells(values):
    grids, grid_side, _, channels = values.shape
    half_side = grid_side // 2
    return values.reshape(grids, half_side, 2, half_side, 2, channels).mean(axis=(2, 4))


def spread_cells(grad_pooled):
    grids, half_side, _, channels = grad_pooled.shape
    quarter = (grad_pooled * 0.25)[:, :, None, :, None, :]
    return jnp.broadcast_to(quarter, (grids, half_side, 2, half_side, 2, channels)).reshape(
        grids, 2 * half_side, 2 * half_side, channels
    )


def on_device(
    patches,
    grid_counts,
    reduce_w,
    conv_w,
    expand_w,
    norm_gain,
    norm_bias,
    readout_w,
    readout_b,
    out_grad,
):
    is_first = lax.axis_index("section") == 0
    capacity = patches.shape[0]
    per_micro = capacity // MICRO
    grid_side = patches.shape[1]
    half_side = grid_side // 2
    channels = patches.shape[3]
    readout_width = readout_w.shape[1]
    middle = reduce_w.shape[2]
    weights = (reduce_w[0], conv_w[0], expand_w[0])
    norm_gains = norm_gain[0]
    norm_biases = norm_bias[0]
    live_grids = jnp.sum(grid_counts)
    slot_mask = (jnp.arange(capacity) < live_grids).astype(jnp.float32)
    empty_send = jnp.zeros((per_micro, half_side, half_side, channels), jnp.bfloat16)
    empty_out = jnp.zeros((per_micro, half_side, half_side, readout_width), jnp.bfloat16)
    empty_grid = jnp.zeros((per_micro, grid_side, grid_side, channels), jnp.bfloat16)
    empty_grads = (
        jnp.zeros((channels, middle), jnp.float32),
        jnp.zeros((9 * middle, middle), jnp.float32),
        jnp.zeros((middle, channels), jnp.float32),
        jnp.zeros((4 * middle + 2 * channels,), jnp.float32),
    )

    def batch_mask(batch):
        return slot_mask[batch * per_micro : (batch + 1) * per_micro][:, None, None, None]

    def second_head(pooled_low):
        block_out, saved = block_forward(pooled_low, weights, norm_gains, norm_biases)
        block_low = block_out.astype(jnp.bfloat16)
        readout_pre = (
            jnp.einsum("gijd,dr->gijr", block_low, readout_w, preferred_element_type=jnp.float32)
            + readout_b
        )
        return (saved, block_low, readout_pre)

    sending = empty_send
    kept_inputs = []
    outputs = []
    for step_index in range(MICRO + 1):
        first_batch = step_index
        second_batch = step_index - 1
        arrived = empty_send
        if step_index > 0:
            arrived = from_behind(sending, "section", 1)
            kept_inputs.append(arrived)

        def forward_first(arrived):
            if first_batch < MICRO:
                grids = patches[first_batch * per_micro : (first_batch + 1) * per_micro]
                block_out, _ = block_forward(grids, weights, norm_gains, norm_biases)
                return (pool_cells(block_out).astype(jnp.bfloat16), empty_out)
            return (empty_send, empty_out)

        def forward_second(arrived):
            if second_batch >= 0:
                _, _, readout_pre = second_head(arrived)
                produced = jax.nn.gelu(readout_pre, approximate=False) * batch_mask(second_batch)
                return (empty_send, produced.astype(jnp.bfloat16))
            return (empty_send, empty_out)

        sending, produced = lax.cond(is_first, forward_first, forward_second, arrived)
        if second_batch >= 0:
            outputs.append(produced)
    mixed_full = jnp.concatenate(outputs, axis=0)
    block_total = empty_grads
    readout_total = (
        jnp.zeros((channels, readout_width), jnp.float32),
        jnp.zeros((readout_width,), jnp.float32),
    )
    returning = empty_send
    input_grads = [empty_grid] * MICRO
    for step_index in range(MICRO + 1):
        second_batch = MICRO - 1 - step_index
        first_batch = MICRO - step_index
        arrived = empty_send
        if step_index > 0:
            arrived = from_behind(returning, "section", -1)

        def backward_first(arrived, readout_now):
            if first_batch < MICRO:
                grids = patches[first_batch * per_micro : (first_batch + 1) * per_micro]
                _, saved = block_forward(grids, weights, norm_gains, norm_biases)
                grad_out = spread_cells(arrived.astype(jnp.float32))
                grad_inputs, weight_grads = block_backward(
                    grids, weights, norm_gains, norm_biases, saved, grad_out
                )
                return (empty_send, grad_inputs.astype(jnp.bfloat16), weight_grads, readout_now)
            return (empty_send, empty_grid, empty_grads, readout_now)

        def backward_second(arrived, readout_now):
            if second_batch >= 0:
                pooled_low = kept_inputs[second_batch]
                saved, block_low, readout_pre = second_head(pooled_low)
                cotangent = out_grad[
                    second_batch * per_micro : (second_batch + 1) * per_micro
                ].astype(jnp.float32) * batch_mask(second_batch)
                _, pullback = jax.vjp(
                    lambda values: jax.nn.gelu(values, approximate=False), readout_pre
                )
                grad_pre = pullback(cotangent)[0].astype(jnp.bfloat16)
                weight_part = jnp.einsum(
                    "gijd,gijr->dr", block_low, grad_pre, preferred_element_type=jnp.float32
                )
                bias_part = jnp.sum(grad_pre.astype(jnp.float32), axis=(0, 1, 2))
                grad_block = jnp.einsum(
                    "gijr,dr->gijd", grad_pre, readout_w, preferred_element_type=jnp.float32
                )
                grad_pooled, weight_grads = block_backward(
                    pooled_low, weights, norm_gains, norm_biases, saved, grad_block
                )
                return (
                    grad_pooled.astype(jnp.bfloat16),
                    empty_grid,
                    weight_grads,
                    (readout_now[0] + weight_part, readout_now[1] + bias_part),
                )
            return (empty_send, empty_grid, empty_grads, readout_now)

        returning, grid_piece, weight_grads, readout_total = lax.cond(
            is_first, backward_first, backward_second, arrived, readout_total
        )
        if step_index > 0:
            input_grads[first_batch] = grid_piece
        block_total = jax.tree.map(jnp.add, block_total, weight_grads)
    block_total = (
        lax.psum_scatter(block_total[0], "dp", scatter_dimension=0, tiled=True),
        lax.psum_scatter(block_total[1], "dp", scatter_dimension=1, tiled=True),
        lax.psum_scatter(block_total[2], "dp", scatter_dimension=1, tiled=True),
        lax.psum_scatter(block_total[3], "dp", scatter_dimension=0, tiled=True),
    )
    readout_grad, bias_grad = readout_total
    readout_part, bias_part = (
        lax.psum_scatter(readout_grad, ("section", "dp"), scatter_dimension=1, tiled=True),
        lax.psum_scatter(bias_grad, ("section", "dp"), scatter_dimension=0, tiled=True),
    )
    grad_scale = 1.0 / lax.axis_size("dp")
    upper_half = from_behind(mixed_full[..., : readout_width // 2], "section", -1)
    mixed = jnp.where(is_first, upper_half, mixed_full[..., readout_width // 2 :])
    grads_full = jnp.concatenate(input_grads, axis=0)
    lower_half = from_behind(grads_full[..., channels // 2 :], "section", 1)
    patch_grad = jnp.where(is_first, grads_full[..., : channels // 2], lower_half)
    return (
        mixed,
        patch_grad,
        (block_total[0] * grad_scale)[None],
        (block_total[1] * grad_scale)[None],
        (block_total[2] * grad_scale)[None],
        (block_total[3] * grad_scale)[None],
        readout_part * grad_scale,
        bias_part * grad_scale,
    )


def solution(mesh):
    placed = (
        P("dp", None, None, None),
        P("dp"),
        P("section", None, None),
        P("section", None, None, None),
        P("section", None, None),
        P("section", None),
        P("section", None),
        P(),
        P(),
        P("dp", None, None, None),
    )
    return jax.shard_map(
        on_device,
        mesh=mesh,
        in_specs=placed,
        out_specs=(
            P("dp", None, None, "section"),
            P("dp", None, None, "section"),
            P("section", "dp", None),
            P("section", None, "dp"),
            P("section", None, "dp"),
            P("section", "dp"),
            P(None, ("section", "dp")),
            P(("section", "dp")),
        ),
        check_vma=False,
    )
```

profile of v0, /device:TPU:0, one launch (start us, length us, event | category | flops | bytes accessed | tf_op | source)
XLA Modules:
  0.0 2027.7 jit_solution(6821955365617394282)
XLA Ops:
  7.2 50.5 %conditional.6 = (bf16[1,12,12,1024]{3,2,1,0:T(8,128)(2,1)S(1)}) conditional(s32[]{:T(128)} %convert_element_type.267, () %tuple.210, (bf16[2,24,24,1024]{3,2,1,0:T(8,128)(2,1)}, bf16[1024,1024]{1,0:T(8,128)(2,1)}, f32[3072]{0:T(1024)}, f32[3072]{0:T(1024)}, bf16[9,1024,1024]{2,1,0:T(8,128)(2,1)}, /*index=5*/bf16[1024,1024]{1,0:T(8,128)(2,1)}) %tuple.438), branch_computations={%region_0.0_spmd, %region_1.9_spmd} | conditional | flops 13321913344 | bytes 201770336 | solution.py:210
  37.4 7.3 fusion.1234
  60.5 64.7 %conditional.7 = (bf16[1,12,12,1024]{3,2,1,0:T(8,128)(2,1)}, bf16[1,12,12,4096]{3,0,2,1:T(2,128)(2,1)S(1)}) conditional(s32[]{:T(128)} %convert_element_type.267, (bf16[1,12,12,1024]{3,2,1,0:T(8,128)(2,1)}, bf16[1024,1024]{1,0:T(8,128)(2,1)}, f32[3072]{0:T(1024)}, f32[3072]{0:T(1024)}, bf16[9,1024,1024]{2,1,0:T(8,128)(2,1)}, ...), branch_computations={%region_9.16_spmd, %region_16.24_spmd} | conditional | flops 13321913344 | bytes 202950000 | solution.py:210
  101.7 7.3 fusion.1244
  128.2 40.0 %conditional.9 = (bf16[1,12,12,1024]{3,2,1,0:T(8,128)(2,1)}, f32[6144]{0:T(1024)S(1)}, f32[1024,4096]{1,0:T(8,128)}, f32[4096]{0:T(1024)}, f32[1024,1024]{1,0:T(...) conditional(s32[]{:T(128)} %convert_element_type.267, (bf16[1,12,12,1024]{3,2,1,0:T(8,128)(2,1)}, ...), branch_computations={%region_32.53_spmd, %region_53.54_spmd} | conditional | flops 13663414272 | bytes 438243456 | solution.py:268
  147.5 7.9 broadcast_in_dim.117
  155.4 12.8 broadcast_in_dim.115.clone
  169.4 158.8 %collective-permute-done.3 = bf16[1,12,12,1024]{3,2,1,0:T(8,128)(2,1)} collective-permute-done((bf16[1,12,12,1024]{3,2,1,0:T(8,128)(2,1)}, bf16[1,12,12,1024]{3,2,1,0:T(8,128)(2,1)}, u32[]{:S(2)}, u32[]{:S(2)}) %collective-permute-start.3) | collective-permute-done | bytes 294944 | tf_op jit(solution)/shard_map/ppermute | solution.py:15
  328.2 298.8 %conditional.10 = (bf16[1,12,12,1024]{3,2,1,0:T(8,128)(2,1)}, bf16[1,24,24,1024]{3,2,1,0:T(8,128)(2,1)}, f32[6144]{0:T(1024)}, f32[1024,4096]{1,0:T(8,128)}, f32...) conditional(s32[]{:T(128)} %convert_element_type.267, ...), branch_computations={%region_54.75_spmd, %region_75.95_spmd} | conditional | flops 39963828224 | bytes 624287296 | solution.py:268
  378.1 8.0 fusion.1270
  410.8 12.4 scatter-add.109
  423.2 7.8 add_select_fusion
  430.9 12.5 scatter-add.112
  443.4 5.5 fusion.914
  449.0 5.4 slice_add_fusion.4
  454.4 11.0 scatter-add.114
  465.5 5.7 slice_add_fusion.3
  471.2 11.0 scatter-add.117
  482.3 5.5 fusion.913
  487.8 5.4 slice_add_fusion.1
  493.2 11.0 scatter-add.119
  504.2 5.7 slice_add_fusion
  510.0 11.0 scatter-add.122
  542.2 11.8 copy.186
  588.9 36.8 %copy.61 = f32[9216,1024]{0,1:T(8,128)} copy(f32[9216,1024]{1,0:T(8,128)} %bitcast.369) | data formatting | bytes 75497472 | tf_op jit(solution)/shard_map/cond | solution.py:268
  630.8 270.0 %conditional.11 = (bf16[1,24,24,1024]{3,2,1,0:T(8,128)(2,1)}, f32[1024,1024]{0,1:T(8,128)}, f32[6144]{0:T(1024)}, f32[9216,1024]{0,1:T(8,128)}, f32[1024,1024]{0,1:T(8,128)}) conditional(s32[]{:T(128)} %convert_element_type.267, () %tuple.215, (bf16[1,12,12,1024]{3,2,1,0:T(8,128)(2,1)S(1)}, bf16[2,24,24,1024]{3,2,1,0:T(8,128)(2,1)}, ...), branch_computations={%region_95.96_spmd, %region_96.116_spmd} | conditional | flops 39963828224 | bytes 572612032 | solution.py:268
  670.4 7.9 fusion.1277
  703.0 12.4 scatter-add.124
  715.3 7.7 add_select_fusion.1
  723.0 12.5 scatter-add.127
  735.5 5.5 fusion.1066
  746.4 11.0 scatter-add.129
  757.5 5.7 slice_add_fusion.9
  763.2 11.0 scatter-add.132
  774.3 5.5 fusion.1065
  785.2 11.0 scatter-add.134
  796.2 5.7 slice_add_fusion.6
  801.9 11.0 scatter-add.137
  863.9 36.8 %copy.65 = f32[9216,1024]{0,1:T(8,128)} copy(f32[9216,1024]{1,0:T(8,128)} %bitcast.443) | data formatting | bytes 75497472 | tf_op jit(solution)/shard_map/cond | solution.py:268
  900.8 8.5 add_add_fusion.17
  909.4 5.4 copy.41
  914.8 8.9 add_add_fusion.18
  924.5 50.3 %add_add_fusion.16 = f32[9216,1024]{0,1:T(8,128)} fusion(f32[9216,1024]{0,1:T(8,128)} %get-tuple-element.770, f32[9216,1024]{0,1:T(8,128)} %get-tuple-element.765, f32[9216,1024]{0,1:T(8,128)} %get-tuple-element.768), kind=kLoop, calls=%fused_computation.1304 | loop fusion | flops 18874368 | bytes 150994944 | tf_op jit(solution)/shard_map/add | solution.py:273
  976.4 7.6 conditional.8
  1001.2 44.2 %all-reduce.13 = f32[4096]{0:T(1024)S(1)} all-reduce(f32[4096]{0:T(1024)} %get-tuple-element.693), channel_id=7, replica_groups=mesh['section'=2,'dp'=16] {'section','dp'}, use_global_device_ids=true, to_apply=%region_121.122.clone | all-reduce | flops 4096 | bytes 32768
  1047.3 78.9 %all-reduce.12 = f32[6144]{0:T(1024)} all-reduce(f32[6144]{0:T(1024)} %add_add_fusion.19), channel_id=5, replica_groups=mesh['section'=2,'dp'=16] {'dp'}, use_global_device_ids=true, to_apply=%region_119.120.clone | all-reduce | flops 6144 | bytes 49152
  1137.4 329.3 %reduce-scatter.11.cloned.1.call-done = f32[1024,128]{1,0:T(8,128)} async-done(((f32[1024,4096]{1,0:T(8,128)}), f32[1024,128]{1,0:T(8,128)}) %reduce-scatter.11.cloned.1.call-update) | async-done | bytes 524304 | tf_op jit(solution)/shard_map/reduce_scatter | solution.py:282
  1468.6 548.9 %reduce-scatter.7.cloned.1.call-done = f32[9216,64]{0,1:T(8,128)} async-done(((f32[9216,1024]{0,1:T(8,128)}), f32[9216,64]{0,1:T(8,128)}) %reduce-scatter.7.cloned.1.call-update) | async-done | bytes 2359312 | tf_op jit(solution)/shard_map/reduce_scatter | solution.py:276
  (314 shorter events, 392.1 us)
Async XLA Ops:
  7.2 1126.9 %reduce-scatter.9.cloned.1.call-start = ((), (), s32[]{:S(2)}) async-start(), calls=%async_computation.6 | async-start | bytes 4456448 | tf_op jit(solution)/shard_map/reduce_scatter | solution.py:277
  7.2 53.2 %copy-start.98 = (f32[4096]{0:T(1024)S(1)}, f32[4096]{0:T(1024)}, u32[]{:S(2)}) copy-start(f32[4096]{0:T(1024)} %param.102) | copy-start | bytes 49156
  11.9 7.0 copy-start.5
  48.5 1.7 copy-start.44
  57.7 2.8 collective-permute-start
  60.4 67.8 %copy-start.104 = (f32[2]{0:T(128)}, f32[2]{0:T(128)S(1)}, u32[]{:S(2)}) copy-start(f32[2]{0:T(128)S(1)} %compare_convert_fusion) | copy-start | bytes 28
  76.1 7.0 copy-start.7
  112.8 1.7 copy-start.45
  125.2 3.0 copy-start.18
  125.2 3.0 collective-permute-start.1
  168.1 160.1 %copy-start.74 = (f32[6144]{0:T(1024)}, f32[6144]{0:T(1024)S(1)}, u32[]{:S(2)}) copy-start(f32[6144]{0:T(1024)S(1)} %get-tuple-element.689) | copy-start | bytes 73732
  168.1 160.1 %collective-permute-start.3 = (bf16[1,12,12,1024]{3,2,1,0:T(8,128)(2,1)}, bf16[1,12,12,1024]{3,2,1,0:T(8,128)(2,1)}, u32[]{:S(2)}, u32[]{:S(2)}) collective-permute-start(bf16[1,12,12,1024]{3,2,1,0:T(8,128)(2,1)} %get-tuple-element.676), channel_id=1, source_target_pairs={{16,0},{17,1},{18,2},{19,3},{20,4},{21,5},{22,6},{23,7},{24,8},{25... | collective-permute-start | bytes 884744 | tf_op jit(solution)/shard_map/ppermute | solution.py:15
  344.9 4.1 copy-start.3
  349.0 8.2 copy-start.10
  351.9 22.4 %copy-start.13 = (f32[24,24,1024]{2,1,0:T(8,128)}, f32[24,24,1024]{2,1,0:T(8,128)S(1)}, u32[]{:S(2)}) copy-start(f32[24,24,1024]{2,1,0:T(8,128)S(1)} %get-tuple-element.953) | copy-start | bytes 7077892 | tf_op jit(solution)/shard_map/cond
  389.9 1.7 copy-start.26
  398.7 5.7 copy-start.48
  443.4 5.6 copy-start.49
  482.2 5.5 copy-start.50
  521.0 4.2 copy-start.14
  525.2 1.7 copy-start.27
  526.9 6.1 copy-start.46
  542.2 11.8 copy-start.51
  565.4 3.8 copy-start.15
  627.0 3.8 collective-permute-start.4
  636.9 4.3 copy-start.4
  641.2 8.2 copy-start.11
  644.1 22.4 %copy-start.16 = (f32[24,24,1024]{2,1,0:T(8,128)}, f32[24,24,1024]{2,1,0:T(8,128)S(1)}, u32[]{:S(2)}) copy-start(f32[24,24,1024]{2,1,0:T(8,128)S(1)} %get-tuple-element.973) | copy-start | bytes 7077892 | tf_op jit(solution)/shard_map/cond
  682.1 1.7 copy-start.28
  690.9 5.7 copy-start.52
  735.5 5.6 copy-start.53
  774.3 5.5 copy-start.54
  813.0 4.4 copy-start.17
  817.3 1.7 copy-start.29
  819.0 6.0 copy-start.47
  825.0 3.9 copy-start.55
  909.4 226.4 %reduce-scatter.5.cloned.1.call-start = ((), (), s32[]{:S(2)}) async-start(), calls=%async_computation.4 | async-start | bytes 4456448 | tf_op jit(solution)/shard_map/reduce_scatter | solution.py:275
  923.7 543.0 %reduce-scatter.11.cloned.1.call-start = ((), (), s32[]{:S(2)}) async-start(), calls=%async_computation.7 | async-start | bytes 17301504 | tf_op jit(solution)/shard_map/reduce_scatter | solution.py:282
  924.4 1093.1 %reduce-scatter.7.cloned.1.call-start = ((), (), s32[]{:S(2)}) async-start(), calls=%async_computation.5 | async-start | bytes 40108032 | tf_op jit(solution)/shard_map/reduce_scatter | solution.py:276
  974.8 1.6 copy-start
  974.8 1.6 copy-start.56
  974.8 1.6 copy-start.57
  984.0 5.0 copy-start.20
  989.0 138.5 %collective-permute-start.2 = (bf16[2,12,12,2048]{3,0,2,1:T(2,128)(2,1)}, bf16[2,12,12,2048]{3,0,2,1:T(2,128)(2,1)S(1)}, u32[]{:S(2)}, u32[]{:S(2)}) collective-permute-start(bf16[2,12,12,2048]{3,0,2,1:T(2,128)(2,1)} %fusion.1210), channel_id=1, source_target_pairs={{16,0},{17,1},{18,2},{19,3},{20,4},{21,5},{22,6},{23,7},{24,8},{25... | collective-permute-start | bytes 3538952 | tf_op jit(solution)/shard_map/ppermute | solution.py:15
  991.7 8.3 copy-start.103
  991.7 135.9 %copy-start.19 = (bf16[1,12,12,4096]{3,0,2,1:T(2,128)(2,1)S(1)}, bf16[1,12,12,4096]{3,0,2,1:T(2,128)(2,1)}, u32[]{:S(2)}) copy-start(bf16[1,12,12,4096]{3,0,2,1:T(2,128)(2,1)} %copy-done.18) | copy-start | bytes 3538948
  995.8 137.1 %collective-permute-start.5 = (bf16[2,24,24,512]{3,2,1,0:T(8,128)(2,1)}, bf16[2,24,24,512]{3,2,1,0:T(8,128)(2,1)}, u32[]{:S(2)}, u32[]{:S(2)}) collective-permute-start(bf16[2,24,24,512]{3,2,1,0:T(8,128)(2,1)} %slice.1979), channel_id=1, source_target_pairs={{0,16},{1,17},{2,18},{3,19},{4,20},{5,21},{6,22},{7,23},{8,24},{9,... | collective-permute-start | bytes 3538952 | tf_op jit(solution)/shard_map/ppermute | solution.py:15
  1127.5 5.3 copy-start.33
  (7 other events, 11.0 us)
Sparse Core Ops, SparseCore 0:
  909.5 97.7 reduce-scatter.8
  1009.6 97.5 reduce-scatter.4
  1109.5 357.1 reduce-scatter.10
  1472.6 544.8 reduce-scatter.6
where the time goes:
time: 2040 us; the launch traced here: 2030 us
  waiting for transfers between devices  1040 us (51%)
  matrix products  336 us (16%)
  local copies, waits for them, and re-layouts  328 us (16%)
  other arithmetic  131 us (6%)
  blocking collectives  123 us (6%)
  loops' own time  40.9 us (2%)
    reduce_scatter x1, waiting for transfers between devices, on_device(): lax.psum_scatter(block_total[1], 'dp', scatter_dimension=1, tiled=True)  549 us
    reduce_scatter x1, waiting for transfers between devices, on_device(): lax.psum_scatter(readout_grad, ('section', 'dp'), scatter_dimension=1, ti...  329 us
    ppermute x6, waiting for transfers between devices, from_behind(): return lax.ppermute(x, axis, pairs)  162 us
    scatter-add x14, local copies, waits for them, and re-layouts, conv_backward(): grad_padded = grad_padded.at[:, vertical:vertical + grid_side, lateral:la...  143 us
    dot_general x36, matrix products, conv_forward(): jnp.einsum('gijc,cd->gijd', window, conv_weights[tap_index], preferred_el...  125 us
    unnamed x2, blocking collectives  123 us
    dot_general x18, matrix products, conv_backward(): jnp.einsum('gijd,cd->gijc', grad_low, conv_weights[tap_index], preferred_...  93.4 us
    cond x4, local copies, waits for them, and re-layouts, on_device(): lax.cond(is_first, backward_first, backward_second, arrived, readout_total)  84.4 us
  transfers between devices with their start and end apart: 10, of which 5 were waited for; matrix products, arithmetic and copies ran while one was open for 5% of the time, Pallas kernels for 0%

commit v1 on v0

v1 whole, which is shorter than its diff:
```python
import functools

import jax
import jax.numpy as jnp
from jax import lax
from jax.experimental import pallas as pl
from jax.experimental.pallas import tpu as pltpu
from jax.sharding import PartitionSpec as P

BF = jnp.bfloat16
F32 = jnp.float32
EPSILON = 1e-05
VMEM_BYTES = 60 * 2**20
READOUT_TILE = 512


def dot_nn(a, b):
    return lax.dot_general(a, b, (((1,), (0,)), ((), ())), preferred_element_type=F32)


def dot_nt(a, b):
    return lax.dot_general(a, b, (((1,), (1,)), ((), ())), preferred_element_type=F32)


def norm_stats(h):
    mean = jnp.mean(h, axis=-1, keepdims=True)
    centered = h - mean
    var = jnp.mean(centered * centered, axis=-1, keepdims=True)
    inv = lax.rsqrt(var + EPSILON)
    return centered * inv, inv


def norm_act(h, gain, bias):
    n, _ = norm_stats(h)
    o = n * gain + bias
    return 0.5 * o * (1.0 + jnp.tanh(0.5 * o))


def norm_pull(dy, h, gain, bias):
    n, inv = norm_stats(h)
    o = n * gain + bias
    s = 0.5 + 0.5 * jnp.tanh(0.5 * o)
    t = dy * (s * (1.0 + o * (1.0 - s)))
    tg = t * gain
    mean_tg = jnp.mean(tg, axis=-1, keepdims=True)
    mean_tgn = jnp.mean(tg * n, axis=-1, keepdims=True)
    return (tg - mean_tg - n * mean_tgn) * inv, t, t * n


def row_loop(rows, body, step=16, unroll=12):
    count = rows // step
    while count % unroll:
        unroll -= 1

    def run(i, carry):
        body(pl.multiple_of(i * step, step))
        return carry

    lax.fori_loop(0, count, run, 0, unroll=unroll)


def fold8(v):
    return jnp.sum(v.reshape(v.shape[0] // 8, 8, v.shape[1]), axis=0)


class Geometry:
    def __init__(self, grids, side, extra=0):
        self.grids = grids
        self.side = side
        self.stride = grids * side
        self.rows = self.stride * side
        self.split = self.stride % 16 != 0
        self.copies = 2 if self.split else 1
        self.extra = extra
        self.padded = self.rows + 2 * self.stride + extra

    def tap_shape(self, channels):
        return (3 * self.copies, self.padded, channels)

    def tap(self, taps, u, v, rows=None):
        rows = self.rows if rows is None else rows
        if not self.split:
            return taps[v, pl.ds(pl.multiple_of(u * self.stride, 16), rows), :]
        middle = (u == 1).astype(jnp.int32)
        start = pl.multiple_of((1 - middle) * u * self.stride, 16)
        return taps[middle * 3 + v, pl.ds(start, rows), :]

    def fill(self, flat, taps):
        channels = taps.shape[-1]
        width = 256
        chunk = 48
        for copy in range(self.copies):
            first = copy * self.stride
            count = (self.padded - 2 * first) // chunk

            def run(k, carry):
                row = pl.multiple_of(k * chunk, chunk)
                for column in range(0, channels, width):
                    c = pl.ds(column, width)
                    a = flat[pl.ds(pl.multiple_of(first + row, 8), chunk), c]
                    j = lax.broadcasted_iota(jnp.int32, a.shape, 0) % self.side
                    r = pl.ds(row, chunk)
                    taps[3 * copy, r, c] = jnp.where(j == 0, 0.0, pltpu.roll(a, 1, 0)).astype(BF)
                    taps[3 * copy + 1, r, c] = a.astype(BF)
                    taps[3 * copy + 2, r, c] = jnp.where(
                        j == self.side - 1, 0.0, pltpu.roll(a, chunk - 1, 0)
                    ).astype(BF)
                return carry

            lax.fori_loop(0, count, run, 0, unroll=1)

    def clear(self, flat):
        flat[pl.ds(0, self.stride), :] = jnp.zeros((self.stride, flat.shape[-1]), flat.dtype)
        tail = self.stride + self.extra
        flat[pl.ds(self.stride + self.rows, tail), :] = jnp.zeros((tail, flat.shape[-1]), flat.dtype)


def constant(shape):
    return pl.BlockSpec(shape, lambda t: (0,) * len(shape), pipeline_mode=pl.Buffered(1))


ANY = pl.BlockSpec(memory_space=pl.ANY)


def copies_out(pairs, sems):
    return [pltpu.make_async_copy(src, dst, sems.at[i]) for i, (src, dst) in enumerate(pairs)]


def first_forward_kernel(
    geo, x_ref, wr_ref, wc_ref, we_ref, gain_ref, bias_ref,
    a1_out, a2_out, h1_out, h2_out, h3_out, z_ref,
    taps, flat, h1, h2, h3, a2, zf, sems,
):
    t = pl.program_id(0)
    on = lax.axis_index("section") == 0
    rows, stride, side = geo.rows, geo.stride, geo.side
    gain = [gain_ref[k : k + 1, :] for k in range(3)]
    bias = [bias_ref[k : k + 1, :] for k in range(3)]
    out = copies_out(
        [(a2, a2_out), (h1, h1_out), (h2, h2_out), (h3, h3_out), (taps.at[1, pl.ds(stride, rows)], a1_out)], sems
    )

    @pl.when(on & (t == 0))
    def _():
        h1[...] = dot_nn(x_ref[...], wr_ref[...])
        out[1].start()
        geo.clear(flat)

        def body(r):
            flat[pl.ds(stride + r, 16), :] = norm_act(h1[pl.ds(r, 16), :], gain[0], bias[0])

        row_loop(rows, body)
        geo.fill(flat, taps)
        out[4].start()
        h2[...] = jnp.zeros_like(h2)

    @pl.when(on & (t >= 1) & (t <= 9))
    def _():
        tap = t - 1
        h2[...] += dot_nn(geo.tap(taps, tap // 3, tap % 3), wc_ref[0])

    @pl.when(on & (t == 10))
    def _():
        out[2].start()

        def body(r):
            a2[pl.ds(r, 16), :] = norm_act(h2[pl.ds(r, 16), :], gain[1], bias[1]).astype(BF)

        row_loop(rows, body)
        out[0].start()
        h3[...] = dot_nn(a2[...], we_ref[...])
        out[3].start()

        def pool(i, carry):
            total = None
            for k in range(2):
                r = pl.ds(pl.multiple_of((2 * i + k) * stride, stride), stride)
                y = x_ref[r, :].astype(F32) + norm_act(h3[r, :], gain[2], bias[2])
                total = y if total is None else total + y
            total = total + pltpu.roll(total, stride - 1, 0)
            pairs = total.reshape(stride // 2, 2, total.shape[1])[:, 0, :]
            zf[pl.ds(pl.multiple_of(i * side, 8), side), :] = pairs * 0.25
            return carry

        lax.fori_loop(0, side // 2, pool, 0, unroll=2)
        z_ref[...] = zf[...].astype(BF)
        for c in out:
            c.wait()


def first_forward(geo, x, wr, wc, we, gain, bias):
    rows, channels = x.shape
    middle = wr.shape[1]
    small = rows // 4
    return pl.pallas_call(
        functools.partial(first_forward_kernel, geo),
        grid=(11,),
        in_specs=[
            constant((rows, channels)), constant((channels, middle)),
            pl.BlockSpec((1, middle, middle), lambda t: (jnp.clip(t - 1, 0, 8), 0, 0)),
            constant((middle, channels)), constant(gain.shape), constant(bias.shape),
        ],
        out_specs=[ANY] * 5 + [constant((small, channels))],
        out_shape=[
            jax.ShapeDtypeStruct((rows, middle), BF), jax.ShapeDtypeStruct((rows, middle), BF),
            jax.ShapeDtypeStruct((rows, middle), F32), jax.ShapeDtypeStruct((rows, middle), F32),
            jax.ShapeDtypeStruct((rows, channels), F32), jax.ShapeDtypeStruct((small, channels), BF),
        ],
        scratch_shapes=[
            pltpu.VMEM(geo.tap_shape(middle), BF), pltpu.VMEM((geo.padded, middle), F32),
            pltpu.VMEM((rows, middle), F32), pltpu.VMEM((rows, middle), F32), pltpu.VMEM((rows, channels), F32),
            pltpu.VMEM((rows, middle), BF), pltpu.VMEM((small, channels), F32), pltpu.SemaphoreType.DMA((5,)),
        ],
        compiler_params=pltpu.CompilerParams(vmem_limit_bytes=VMEM_BYTES),
        cost_estimate=pl.CostEstimate(flops=22 * rows * channels * middle, bytes_accessed=40 * 2**20, transcendentals=0),
        name="first_forward",
    )(x, wr, wc, we, gain, bias)


def second_forward_kernel(
    geo, tiles, live_ref, z_ref, wr_ref, wc_ref, we_ref, gain_ref, bias_ref, wro_ref, rb_ref, og_ref,
    a1_ref, a2_ref, h1, h2, h3, y_ref, dy_ref, mixed_ref, dpre_ref, gb_ref,
    taps, flat,
):
    t = pl.program_id(0)
    on = lax.axis_index("section") == 1
    rows, stride = geo.rows, geo.stride
    gain = [gain_ref[k : k + 1, :] for k in range(3)]
    bias = [bias_ref[k : k + 1, :] for k in range(3)]

    @pl.when(on & (t == 0))
    def _():
        h1[...] = dot_nn(z_ref[...], wr_ref[...])
        geo.clear(flat)

        def body(r):
            a = norm_act(h1[pl.ds(r, 16), :], gain[0], bias[0])
            flat[pl.ds(stride + r, 16), :] = a
            a1_ref[pl.ds(r, 16), :] = a.astype(BF)

        row_loop(rows, body)
        geo.fill(flat, taps)
        h2[...] = jnp.zeros_like(h2)

    @pl.when(on & (t >= 1) & (t <= 9))
    def _():
        tap = t - 1
        h2[...] += dot_nn(geo.tap(taps, tap // 3, tap % 3), wc_ref[0])

    @pl.when(on & (t == 10))
    def _():
        def body(r):
            a2_ref[pl.ds(r, 16), :] = norm_act(h2[pl.ds(r, 16), :], gain[1], bias[1]).astype(BF)

        row_loop(rows, body)
        h3[...] = dot_nn(a2_ref[...], we_ref[...])

        def last(r):
            y = z_ref[pl.ds(r, 16), :].astype(F32) + norm_act(h3[pl.ds(r, 16), :], gain[2], bias[2])
            y_ref[pl.ds(r, 16), :] = y.astype(BF)

        row_loop(rows, last)
        dy_ref[...] = jnp.zeros_like(dy_ref)

    @pl.when(on & (t >= 11))
    def _():
        pre = dot_nn(y_ref[...], wro_ref[...]) + rb_ref[...]
        slot = lax.broadcasted_iota(jnp.int32, (rows, 1), 0) % stride // geo.side
        mask = jnp.where(slot < live_ref[0], 1.0, 0.0)
        phi = 0.5 + 0.5 * lax.erf(pre * 0.7071067811865476)
        mixed_ref[...] = (pre * phi * mask).astype(BF)
        density = jnp.exp(-0.5 * pre * pre) * 0.3989422804014327
        low = (og_ref[...].astype(F32) * mask * (phi + pre * density)).astype(BF)
        dpre_ref[...] = low
        gb_ref[...] = jnp.sum(low.astype(F32), axis=0, keepdims=True)
        dy_ref[...] += dot_nt(low, wro_ref[...])


def second_forward(geo, live, z, wr, wc, we, gain, bias, wro, rb, og):
    rows, channels = z.shape
    middle = wr.shape[1]
    units = wro.shape[1]
    tile = READOUT_TILE
    tiles = units // tile

    def at(t):
        return jnp.clip(t - 11, 0, tiles - 1)

    def rowsof(dtype, width=middle):
        return jax.ShapeDtypeStruct((rows, width), dtype)

    return pl.pallas_call(
        functools.partial(second_forward_kernel, geo, tiles),
        grid=(11 + tiles,),
        in_specs=[
            pl.BlockSpec(memory_space=pltpu.SMEM),
            constant((rows, channels)), constant((channels, middle)),
            pl.BlockSpec((1, middle, middle), lambda t: (jnp.clip(t - 1, 0, 8), 0, 0)),
            constant((middle, channels)), constant(gain.shape), constant(bias.shape),
            pl.BlockSpec((channels, tile), lambda t: (0, at(t))),
            pl.BlockSpec((1, tile), lambda t: (0, at(t))),
            pl.BlockSpec((rows, tile), lambda t: (0, at(t))),
        ],
        out_specs=[constant((rows, middle))] * 7
        + [pl.BlockSpec((rows, tile), lambda t: (0, at(t)))] * 2 + [pl.BlockSpec((1, tile), lambda t: (0, at(t)))],
        out_shape=[
            rowsof(BF), rowsof(BF), rowsof(F32), rowsof(F32), rowsof(F32), rowsof(BF), rowsof(F32),
            rowsof(BF, units), rowsof(BF, units), jax.ShapeDtypeStruct((1, units), F32),
        ],
        scratch_shapes=[pltpu.VMEM(geo.tap_shape(middle), BF), pltpu.VMEM((geo.padded, middle), F32)],
        compiler_params=pltpu.CompilerParams(vmem_limit_bytes=VMEM_BYTES),
        cost_estimate=pl.CostEstimate(flops=40 * rows * channels * middle, bytes_accessed=40 * 2**20, transcendentals=0),
        name="second_forward",
    )(live, z, wr, wc, we, gain, bias, wro, rb, og)


def backward_kernel(
    geo, section, pooled, d_ref, h1_in, h2_in, h3_in, wr_ref, wc_ref, we_ref, gain_ref, bias_ref,
    dh3_out, dh2_out, dh1_out, dx_ref, norm_ref,
    taps, flat, h1, h2, h3, low, dy, sems, sems_out,
):
    t = pl.program_id(0)
    on = lax.axis_index("section") == section
    rows, stride, side = geo.rows, geo.stride, geo.side
    gain = [gain_ref[k : k + 1, :] for k in range(3)]
    bias = [bias_ref[k : k + 1, :] for k in range(3)]
    loads = [pltpu.make_async_copy(s, d, sems.at[i]) for i, (s, d) in enumerate([(h3_in, h3), (h2_in, h2), (h1_in, h1)])]
    out3, out2, out1 = copies_out([(low.at[0], dh3_out), (low.at[1], dh2_out), (low.at[2], dh1_out)], sems_out)

    def pull(k, source, h, store):
        norm_ref[k] = jnp.zeros_like(norm_ref[k])
        norm_ref[3 + k] = jnp.zeros_like(norm_ref[k])

        def body(r):
            dh, tt, tn = norm_pull(source[pl.ds(r, 16), :], h[pl.ds(r, 16), :], gain[k], bias[k])
            store(r, dh)
            norm_ref[k] += fold8(tn)
            norm_ref[3 + k] += fold8(tt)

        row_loop(rows, body, unroll=9)

    @pl.when(on & (t == 0))
    def _():
        for c in loads:
            c.start()
        if pooled:
            half = side // 2
            grids = stride // side
            narrow = grids * half
            flat[pl.ds(0, half * narrow), :] = d_ref[...].astype(F32)
            a = lax.broadcasted_iota(jnp.int32, (stride, narrow), 0) // 2
            b = lax.broadcasted_iota(jnp.int32, (stride, narrow), 1)
            quarter = jnp.where(a == b, 0.25, 0.0).astype(BF)

            def widen(i, carry):
                part = flat[pl.ds(pl.multiple_of(i * narrow, 8), narrow), :].astype(BF)
                wide = dot_nn(quarter, part)
                for k in range(2):
                    dy[pl.ds(pl.multiple_of((2 * i + k) * stride, stride), stride), :] = wide
                return carry

            lax.fori_loop(0, half, widen, 0, unroll=2)
        else:
            dy[...] = d_ref[...]
        loads[0].wait()

        def store3(r, v):
            low[0, pl.ds(r, 16), :] = v.astype(BF)

        pull(2, dy, h3, store3)
        out3.start()
        h3[...] = dot_nt(low[0], we_ref[...])
        loads[1].wait()
        geo.clear(flat)

        def store2(r, v):
            low[1, pl.ds(r, 16), :] = v.astype(BF)
            flat[pl.ds(stride + r, 16), :] = v

        pull(1, h3, h2, store2)
        out2.start()
        geo.fill(flat, taps)
        h2[...] = jnp.zeros_like(h2)

    @pl.when(on & (t >= 1) & (t <= 9))
    def _():
        tap = t - 1
        h2[...] += dot_nt(geo.tap(taps, tap // 3, tap % 3), wc_ref[0])

    @pl.when(on & (t == 10))
    def _():
        loads[2].wait()

        def store1(r, v):
            low[2, pl.ds(r, 16), :] = v.astype(BF)

        pull(0, h2, h1, store1)
        out1.start()
        dx_ref[...] = (dy[...] + dot_nt(low[2], wr_ref[...])).astype(BF)
        for c in (out3, out2, out1):
            c.wait()


def backward(geo, section, pooled, d, h1, h2, h3, wr, wc, we, gain, bias):
    rows = geo.rows
    channels, middle = wr.shape
    low = jax.ShapeDtypeStruct((rows, middle), BF)
    return pl.pallas_call(
        functools.partial(backward_kernel, geo, section, pooled),
        grid=(11,),
        in_specs=[
            constant(d.shape), ANY, ANY, ANY, constant((channels, middle)),
            pl.BlockSpec((1, middle, middle), lambda t: (8 - jnp.clip(t - 1, 0, 8), 0, 0)),
            constant((middle, channels)), constant(gain.shape), constant(bias.shape),
        ],
        out_specs=[ANY] * 3 + [constant((rows, channels)), constant((6, 8, channels))],
        out_shape=[low, low, low, jax.ShapeDtypeStruct((rows, channels), BF), jax.ShapeDtypeStruct((6, 8, channels), F32)],
        scratch_shapes=[
            pltpu.VMEM(geo.tap_shape(middle), BF), pltpu.VMEM((geo.padded, middle), F32),
            pltpu.VMEM((rows, middle), F32), pltpu.VMEM((rows, middle), F32), pltpu.VMEM((rows, channels), F32),
            pltpu.VMEM((3, rows, middle), BF), pltpu.VMEM((rows, channels), F32),
            pltpu.SemaphoreType.DMA((3,)), pltpu.SemaphoreType.DMA((3,)),
        ],
        compiler_params=pltpu.CompilerParams(vmem_limit_bytes=VMEM_BYTES),
        cost_estimate=pl.CostEstimate(flops=22 * rows * channels * middle, bytes_accessed=40 * 2**20, transcendentals=0),
        name="backward",
    )(d, h1, h2, h3, wr, wc, we, gain, bias)


class Scatter:
    def __init__(self, size, rows):
        self.size = size
        self.bits = size.bit_length() - 1
        self.block = max(rows // size, 16)
        self.low = (self.block * size // rows).bit_length() - 1
        self.high = self.bits - self.low

    def exchange(self, x, bit):
        return lax.ppermute(x, "dp", [(i, i ^ (1 << bit)) for i in range(self.size)])

    def run(self, send, keep, order):
        units, _, columns = send.shape
        left = [b for b in reversed(range(self.high)) if b != order[0]]
        shape = (units,) + (2,) * len(left) + (self.block, columns)
        send, keep = send.reshape(shape), keep.reshape(shape)
        for step, bit in enumerate(order):
            got = self.exchange(send, bit + self.low)
            if step + 1 == len(order):
                total = got.astype(F32) + keep.astype(F32)
                break
            axis = 1 + left.index(order[step + 1])
            left.remove(order[step + 1])

            def half(v, k):
                return lax.index_in_dim(v, k, axis, keepdims=False).astype(F32)

            send = (half(got, 1) + half(keep, 1)).astype(BF)
            keep = half(got, 0) + half(keep, 0)
        total = total.reshape(units, self.block, columns)
        for bit in reversed(range(self.low)):
            pair = total.reshape(units, 2, total.shape[1] // 2, columns)
            mine = (lax.axis_index("dp") >> bit) & 1
            send = jnp.where(mine == 0, pair[:, 1], pair[:, 0])
            total = jnp.where(mine == 0, pair[:, 0], pair[:, 1])
            total = total + self.exchange(send.astype(BF), bit).astype(F32)
        return total


def turn(lhs, turned, block, flip):
    def run(q, carry):
        part = jnp.transpose(lhs[:, pl.ds(pl.multiple_of(q * 128, 128), 128)])
        step = min(block, 128)
        for s in range(128 // step):
            row = q * 128 + s * step
            target = ((row // block) ^ flip) * block + row % block
            turned[pl.ds(pl.multiple_of(target, 16), step), :] = part[s * step : (s + 1) * step]
        return carry

    lax.fori_loop(0, lhs.shape[1] // 128, run, 0, unroll=1)


def store_halves(value, send, keep, block, bit):
    run = block << bit
    for i in range(value.shape[0] // run):
        target = keep if i % 2 == 0 else send
        target[0, pl.ds(i // 2 * run, run), :] = value[i * run : (i + 1) * run].astype(BF)


def fetch(own, pairs, sems):
    @pl.when(own)
    def _():
        cs = [pltpu.make_async_copy(a, t, sems.at[i]) for i, (a, b, t) in enumerate(pairs)]
        for c in cs:
            c.start()
        for c in cs:
            c.wait()

    @pl.when(jnp.logical_not(own))
    def _():
        cs = [pltpu.make_async_copy(b, t, sems.at[i]) for i, (a, b, t) in enumerate(pairs)]
        for c in cs:
            c.start()
        for c in cs:
            c.wait()


GROUPS = ((0, 4, 0), (4, 4, 1), (8, 3, 2))


def block_grads_kernel(
    geo, section, scatter, *refs
):
    names = ("a1", "a2", "dh3", "dh2", "dh1")
    own_refs, got_refs = refs[0:5], refs[5:10]
    x_ref = refs[10]
    outs = refs[11:17]
    right, wide, flat, taps, turned, sems = refs[17:]
    own = lax.axis_index("section") == section
    mine = lax.axis_index("section")
    flip = lax.axis_index("dp") // (1 << scatter.low)
    t = pl.program_id(0)
    rows, stride = geo.rows, geo.stride
    depth = wide.shape[0]
    width = right.shape[1]
    columns = pl.ds(pl.multiple_of(mine * width, width), width)

    def load(right_name, wide_name):
        k = names.index(right_name)
        pairs = [(own_refs[k].at[:, columns], got_refs[k].at[:, columns], right.at[pl.ds(0, rows)])]
        if wide_name is not None:
            j = names.index(wide_name)
            pairs.append((own_refs[j], got_refs[j], wide.at[pl.ds(0, rows)]))
        else:
            pairs.append((x_ref, x_ref, wide.at[pl.ds(0, rows)]))
        fetch(own, pairs, sems)

    def emit(value, group):
        store_halves(value, outs[2 * group], outs[2 * group + 1], scatter.block, GROUPS[group][2])

    @pl.when(t == 0)
    def _():
        if depth > rows:
            wide[pl.ds(rows, depth - rows), :] = jnp.zeros((depth - rows, wide.shape[1]), BF)
            right[pl.ds(rows, depth - rows), :] = jnp.zeros((depth - rows, width), BF)
        load("a1", "dh2")
        geo.clear(flat)

        def body(r):
            flat[pl.ds(stride + r, 16), :] = right[pl.ds(r, 16), :].astype(F32)

        row_loop(rows, body)
        geo.fill(flat, taps)
        turn(wide, turned, scatter.block, flip)

    for group, (first, count, _) in enumerate(GROUPS):
        @pl.when((t >= first) & (t < min(first + count, 9)))
        def _():
            value = dot_nn(turned[...], geo.tap(taps, t // 3, t % 3, depth))
            emit(value, group)

    for step, names_used in ((9, ("a2", "dh3")), (10, ("dh1", None))):
        @pl.when(t == step)
        def _():
            load(*names_used)
            turn(wide, turned, scatter.block, flip)
            emit(dot_nn(turned[...], right[...]), 2)


def block_grads(geo, section, size, own, got, x):
    rows, channels = x.shape
    scatter = Scatter(size, channels)
    width = channels // 2
    depth = -(-rows // 128) * 128
    geo = Geometry(geo.grids, geo.side, depth - rows)
    half = channels // 2

    def group_spec(first, count):
        return pl.BlockSpec((1, half, width), lambda t: (jnp.clip(t - first, 0, count - 1), 0, 0))

    specs, shapes = [], []
    for first, count, _ in GROUPS:
        specs += [group_spec(first, count)] * 2
        shapes += [jax.ShapeDtypeStruct((count, half, width), BF)] * 2
    outs = pl.pallas_call(
        functools.partial(block_grads_kernel, geo, section, scatter),
        grid=(11,),
        in_specs=[ANY] * 11,
        out_specs=specs,
        out_shape=shapes,
        scratch_shapes=[
            pltpu.VMEM((depth, width), BF), pltpu.VMEM((depth, channels), BF), pltpu.VMEM((geo.padded, width), F32),
            pltpu.VMEM(geo.tap_shape(width), BF), pltpu.VMEM((channels, depth), BF), pltpu.SemaphoreType.DMA((2,)),
        ],
        compiler_params=pltpu.CompilerParams(vmem_limit_bytes=VMEM_BYTES),
        cost_estimate=pl.CostEstimate(flops=11 * rows * channels * channels, bytes_accessed=20 * 2**20, transcendentals=0),
        name="block_grads",
    )(*own, *got, x)
    orders = {0: [0, 1], 1: [1, 0], 2: [2, 3]}
    results = []
    for g, (_, _, bit) in enumerate(GROUPS):
        head = orders[bit]
        order = head + [b for b in range(scatter.high) if b not in head]
        if bit == 2:
            order = [b for b in range(2, scatter.high)] + [0, 1]
        results.append(scatter.run(outs[2 * g], outs[2 * g + 1], order))
    return jnp.concatenate(results, axis=0)


def readout_grads_kernel(
    rows, scatter, y_own, y_got, d_own, d_got, send0, keep0, send1, keep1, right, wide, turned, sems
):
    own = lax.axis_index("section") == 1
    mine = lax.axis_index("section")
    t = pl.program_id(0)
    depth, width = right.shape
    columns = pl.ds(pl.multiple_of(mine * width, width), width)

    @pl.when(t == 0)
    def _():
        if depth > rows:
            wide[pl.ds(rows, depth - rows), :] = jnp.zeros((depth - rows, wide.shape[1]), BF)
            right[pl.ds(rows, depth - rows), :] = jnp.zeros((depth - rows, width), BF)
        fetch(own, [(y_own.at[:, columns], y_got.at[:, columns], right.at[pl.ds(0, rows)]),
                    (d_own, d_got, wide.at[pl.ds(0, rows)])], sems)
        turn(wide, turned, scatter.block, lax.axis_index("dp"))

    part = turned.shape[0] // 4
    for s, (send, keep) in enumerate(((send0, keep0), (send1, keep1))):
        @pl.when(t // 2 == s)
        def _():
            value = dot_nn(turned[pl.ds(pl.multiple_of(t * part, part), part), :], right[...])
            store_halves(value, send, keep, scatter.block, s)


def readout_grads(size, y_own, y_got, d_own, d_got):
    rows, channels = y_own.shape
    units = d_own.shape[1]
    scatter = Scatter(size, units // 2)
    width = channels // 2
    depth = -(-rows // 128) * 128
    half = units // 8
    out = jax.ShapeDtypeStruct((2, half, width), BF)
    specs = [pl.BlockSpec((1, half, width), lambda t: (jnp.clip(t, 0, 1), 0, 0))] * 2
    specs += [pl.BlockSpec((1, half, width), lambda t: (jnp.clip(t - 2, 0, 1), 0, 0))] * 2
    outs = pl.pallas_call(
        functools.partial(readout_grads_kernel, rows, scatter),
        grid=(4,),
        in_specs=[ANY] * 4,
        out_specs=specs,
        out_shape=[out] * 4,
        scratch_shapes=[
            pltpu.VMEM((depth, width), BF), pltpu.VMEM((depth, units), BF), pltpu.VMEM((units, depth), BF),
            pltpu.SemaphoreType.DMA((2,)),
        ],
        compiler_params=pltpu.CompilerParams(vmem_limit_bytes=VMEM_BYTES),
        cost_estimate=pl.CostEstimate(flops=rows * channels * units, bytes_accessed=12 * 2**20, transcendentals=0),
        name="readout_grads",
    )(y_own, y_got, d_own, d_got)
    rest = list(range(2, scatter.high))
    results = []
    for s, head in enumerate(([0, 1], [1, 0])):
        send, keep = (v.reshape(1, 2 * half, width) for v in outs[2 * s : 2 * s + 2])
        results.append(scatter.run(send, keep, head + rest))
    return jnp.concatenate(results, axis=0)


def to_section(x, target):
    return lax.ppermute(x, "section", [(1 - target, target)])


def swap_sections(x):
    return lax.ppermute(x, "section", [(0, 1), (1, 0)])


def side_by_side(v):
    grids, side, _, channels = v.shape
    return v.transpose(1, 0, 2, 3).reshape(grids * side * side, channels)


def by_grid(v, grids, side):
    return v.reshape(side, grids, side, v.shape[-1]).transpose(1, 0, 2, 3)


def on_device(
    size, patches, grid_counts, reduce_w, conv_w, expand_w, norm_gain, norm_bias, readout_w, readout_b, out_grad
):
    section = lax.axis_index("section")
    is_first = section == 0
    grids, side, _, channels = patches.shape
    middle = reduce_w.shape[2]
    units = readout_w.shape[1]
    wide, small = Geometry(grids, side), Geometry(grids, side // 2)
    weights = (reduce_w[0], conv_w[0], expand_w[0], norm_gain.reshape(3, channels), norm_bias.reshape(3, channels))
    live = jnp.sum(grid_counts, dtype=jnp.int32).reshape(1)
    x = side_by_side(patches)
    cotangent = side_by_side(out_grad)

    a1, a2, h1, h2, h3, z = first_forward(wide, x, *weights)
    z_got = to_section(z, 1)
    z_all = jnp.where(is_first, z, z_got)
    first_got = [to_section(v, 1) for v in (a1, a2)]
    b1, b2, k1, k2, k3, y, dy, mixed_full, dpre, bias_sum = second_forward(
        small, live, z_got, *weights, readout_w, readout_b.reshape(1, units), cotangent
    )
    y_got, dpre_got = to_section(y, 0), to_section(dpre, 0)
    second_got = [to_section(v, 0) for v in (b1, b2)]
    e3, e2, e1, dz, norm_second = backward(small, 1, False, dy, k1, k2, k3, *weights)
    dz_got = to_section(dz, 0)
    second_got += [to_section(v, 0) for v in (e3, e2, e1)]
    readout_part = readout_grads(size, y, y_got, dpre, dpre_got)
    second_part = block_grads(small, 1, size, (b1, b2, e3, e2, e1), second_got, z_all)
    d3, d2, d1, dx, norm_first = backward(wide, 0, True, dz_got, h1, h2, h3, *weights)
    first_got += [to_section(v, 1) for v in (d3, d2, d1)]
    first_part = block_grads(wide, 0, size, (a1, a2, d3, d2, d1), first_got, x)

    scale = 1.0 / size
    block_part = jnp.where(is_first, first_part, second_part)
    other = swap_sections(jnp.where(is_first, second_part, first_part))
    block_total = jnp.where(
        is_first, jnp.concatenate([block_part, other], axis=2), jnp.concatenate([other, block_part], axis=2)
    ) * scale
    rows = block_total.shape[1]
    conv_total = block_total[:9].transpose(0, 2, 1).reshape(1, 9 * middle, rows)
    expand_total = block_total[9].T[None]
    reduce_total = block_total[10][None]
    mine = jnp.where(is_first, readout_part[0], readout_part[1])
    other = swap_sections(jnp.where(is_first, readout_part[1], readout_part[0]))
    readout_total = jnp.where(
        is_first, jnp.concatenate([mine, other], axis=1), jnp.concatenate([other, mine], axis=1)
    ).T * scale

    norms = jnp.where(is_first, norm_first, norm_second).sum(axis=1).reshape(size, -1)
    share = norms.shape[1]
    biases = bias_sum.reshape(2, size, -1)
    vectors = jnp.concatenate([norms, biases[0], biases[1]], axis=1)
    vectors = lax.psum_scatter(vectors, "dp", scatter_dimension=0, tiled=True)[0] * scale
    count = biases.shape[2]
    low = to_section(vectors[share : share + count], 0)
    bias_total = jnp.where(is_first, low, vectors[share + count :])

    low = to_section(mixed_full[:, : units // 2], 0)
    mixed = by_grid(jnp.where(is_first, low, mixed_full[:, units // 2 :]), grids, side // 2)
    high = to_section(dx[:, channels // 2 :], 1)
    patch_grad = by_grid(jnp.where(is_first, dx[:, : channels // 2], high), grids, side)
    return (
        mixed, patch_grad, reduce_total, conv_total, expand_total, vectors[None, :share], readout_total, bias_total,
    )


def solution(mesh):
    size = mesh.shape["dp"]
    placed = (
        P("dp", None, None, None), P("dp"), P("section", None, None), P("section", None, None, None),
        P("section", None, None), P("section", None), P("section", None), P(), P(), P("dp", None, None, None),
    )
    return jax.shard_map(
        functools.partial(on_device, size),
        mesh=mesh,
        in_specs=placed,
        out_specs=(
            P("dp", None, None, "section"), P("dp", None, None, "section"), P("section", "dp", None),
            P("section", None, "dp"), P("section", None, "dp"), P("section", "dp"), P(None, ("section", "dp")),
            P(("section", "dp")),
        ),
        check_vma=False,
    )
```

time: 2040 us -> 663 us (0.33)
  waiting for transfers between devices: 1040 us -> 224 us
  matrix products: 336 us -> 0 us
  local copies, waits for them, and re-layouts: 328 us -> 66 us
  Pallas kernels: 0 us -> 190 us
  other arithmetic: 131 us -> 33.9 us
  starting transfers between devices: 12.2 us -> 63.5 us
  blocking collectives: 123 us -> 74.4 us
  loops' own time: 40.9 us -> 0 us
    reduce_scatter x4 -> x0, waiting for transfers between devices: 878 us -> none  [the longest x1 549 us: on_device(): lax.psum_scatter(block_total[1], 'dp', scatter_dimension=1, tiled=True)]
    dot_general x88 -> x0, matrix products: 336 us -> none  [the longest x36 125 us: conv_forward(): jnp.einsum('gijc,cd->gijd', window, conv_weights[tap_index], preferred_el...]
    pallas_call x0 -> x7, Pallas kernels: none -> 190 us  [the longest x2 66.9 us: backward(): pl.pallas_call(functools.partial(backward_kernel, geo, section, pooled),...]
    scatter-add x14 -> x0, local copies, waits for them, and re-layouts: 143 us -> none  [conv_backward(): grad_padded = grad_padded.at[:, vertical:vertical + grid_side, lateral:la...]
    cond x77 -> x0, local copies, waits for them, and re-layouts: 119 us -> none  [the longest x4 84.4 us: on_device(): lax.cond(is_first, backward_first, backward_second, arrived, readout_total)]
    add x6, other arithmetic: 73.8 us -> 0.56 us  [run(): total = got.astype(F32) + keep.astype(F32)]
    ppermute x6 -> x51, waiting for transfers between devices: 162 us -> 224 us  [the longest x32 204 us: exchange(): return lax.ppermute(x, 'dp', [(i, i ^ 1 << bit) for i in range(self.size)])]
    ppermute x6 -> x51, starting transfers between devices: 12.1 us -> 63.5 us  [the longest x17 34.1 us: to_section(): return lax.ppermute(x, 'section', [(1 - target, target)])]
  transfers between devices with their start and end apart: 10 -> 51, of which waited for: 5 -> 22; matrix products, arithmetic and copies ran while one was open for 5% -> 11% of each run, Pallas kernels for 0% -> 16%
where the time goes in v1:
time: 663 us; the launch traced here: 655 us
  waiting for transfers between devices  224 us (34%)
  Pallas kernels  190 us (29%)
  blocking collectives  74.4 us (11%)
  local copies, waits for them, and re-layouts  66 us (10%)
  starting transfers between devices  63.5 us (10%)
  other arithmetic  33.9 us (5%)
    ppermute x32, waiting for transfers between devices, exchange(): return lax.ppermute(x, 'dp', [(i, i ^ 1 << bit) for i in range(self.size)])  204 us
    unnamed x1, blocking collectives  74.4 us
    pallas_call x2, Pallas kernels, backward(): pl.pallas_call(functools.partial(backward_kernel, geo, section, pooled),...  66.9 us
    pallas_call x2, Pallas kernels, block_grads(): pl.pallas_call(functools.partial(block_grads_kernel, geo, section, scatte...  48.9 us
    pallas_call x1, Pallas kernels, first_forward(): pl.pallas_call(functools.partial(first_forward_kernel, geo), grid=(11,),...  44.3 us
    ppermute x17, starting transfers between devices, to_section(): return lax.ppermute(x, 'section', [(1 - target, target)])  34.1 us
    ppermute x32, starting transfers between devices, exchange(): return lax.ppermute(x, 'dp', [(i, i ^ 1 << bit) for i in range(self.size)])  29.3 us
    convert_element_type x24, other arithmetic, run(): send = (half(got, 1) + half(keep, 1)).astype(BF)  21.7 us
  transfers between devices with their start and end apart: 51, of which 22 were waited for; matrix products, arithmetic and copies ran while one was open for 11% of the time, Pallas kernels for 16%

profile of v1, /device:TPU:0, one launch (start us, length us, event | category | flops | bytes accessed | tf_op | source)
XLA Modules:
  0.0 654.6 jit_solution(8774349618901008995)
XLA Ops:
  0.7 3.4 copy.75
  7.1 44.3 %first_forward.1 = (bf16[1152,1024]{1,0:T(8,128)(2,1)}, bf16[1152,1024]{1,0:T(8,128)(2,1)}, f32[1152,1024]{1,0:T(8,128)}, f32[1152,1024]{1,0:T(8,128)}, f32[1152,1024]{1,0:T(8,128)}, /*index=5*/bf16[288,1024]{1,0:T(8,128)(2,1)}) custom-call(bf16[1152,1024]{1,0:T(8,128)(2,1)} %bitcast.180, bf16[1024,1024]{1,0:T(8,128)(2,1)} %bitcast.191, ...), custom_call_target="tpu_custom_call" | custom-call | flops 26575110144 | bytes 41943040 | tf_op jit(solution)/shard_map/first_forward/pallas_call | solution.py:195
  51.5 2.6 collective-permute-start
  54.7 3.4 copy.76
  60.4 21.0 %second_forward.1 = (bf16[288,1024]{1,0:T(8,128)(2,1)}, bf16[288,1024]{1,0:T(8,128)(2,1)}, f32[288,1024]{1,0:T(8,128)}, f32[288,1024]{1,0:T(8,128)}, f32[288,102...) custom-call(s32[1]{0:T(128)S(6)} %copy.134.live_ref, ...), custom_call_target="tpu_custom_call" | custom-call | flops 12079595520 | bytes 41943040 | tf_op jit(solution)/shard_map/second_forward/pallas_call | solution.py:292
  84.0 11.6 %backward.2 = (bf16[288,1024]{1,0:T(8,128)(2,1)}, bf16[288,1024]{1,0:T(8,128)(2,1)}, bf16[288,1024]{1,0:T(8,128)(2,1)}, bf16[288,1024]{1,0:T(8,128)(2,1)}, f32[6,8,1024]{2,1,0:T(8,128)}) custom-call(f32[288,1024]{1,0:T(8,128)} %get-tuple-element.52.d_ref, f32[288,1024]{1,0:T(8,128)} %get-tuple-element.53.h1_in, f32[288,1024]{1,0:T(8,128)} %get-tuple-element.54.h2_in, ...), custom_call_target="tpu_custom_call" | custom-call | flops 6643777536 | bytes 41943040 | tf_op jit(solution)/shard_map/backward/pallas_call | solution.py:408
  100.4 17.3 %collective-permute-done.23.refs_7_ = bf16[288,1024]{1,0:T(8,128)(2,1)S(1)} collective-permute-done((bf16[288,1024]{1,0:T(8,128)(2,1)}, bf16[288,1024]{1,0:T(8,128)(2,1)S(1)}, u32[]{:S(2)}, u32[]{:S(2)}) %collective-permute-start.23) | collective-permute-done | bytes 589856 | tf_op jit(solution)/shard_map/ppermute | solution.py:668
  121.3 17.8 %block_grads.3 = (bf16[4,512,512]{2,1,0:T(8,128)(2,1)}, bf16[4,512,512]{2,1,0:T(8,128)(2,1)}, bf16[4,512,512]{2,1,0:T(8,128)(2,1)}, bf16[4,512,512]{2,1,0:T(8,12...) custom-call(bf16[288,1024]{1,0:T(8,128)(2,1)} %get-tuple-element.72.refs_0_, ...), custom_call_target="tpu_custom_call" | custom-call | flops 3321888768 | bytes 20971520 | tf_op jit(solution)/shard_map/block_grads/pallas_call | solution.py:584
  139.1 2.9 copy.93
  142.0 3.0 collective-permute-start.34
  154.9 24.7 %collective-permute-done.34 = bf16[3,2,2,2,64,512]{5,4,0,2,3,1:T(8,128)(2,1)} collective-permute-done((bf16[3,2,2,2,64,512]{5,4,0,2,3,1:T(8,128)(2,1)}, bf16[3,2,2,2,64,512]{5,4,0,2,3,1:T(8,128)(2,1)}, u32[]{:S(2)}, u32[]{:S(2)}) %collective-permute-start.34) | collective-permute-done | bytes 1572896 | tf_op jit(solution)/shard_map/ppermute | solution.py:439
  181.8 2.8 fusion.16
  184.6 2.6 collective-permute-start.35
  187.2 55.3 %backward.3 = (bf16[1152,1024]{1,0:T(8,128)(2,1)}, bf16[1152,1024]{1,0:T(8,128)(2,1)}, bf16[1152,1024]{1,0:T(8,128)(2,1)}, bf16[1152,1024]{1,0:T(8,128)(2,1)}, f32[6,8,1024]{2,1,0:T(8,128)}) custom-call(bf16[288,1024]{1,0:T(8,128)(2,1)} %copy-done.37, f32[1152,1024]{1,0:T(8,128)} %get-tuple-element.57.h1_in, f32[1152,1024]{1,0:T(8,128)} %get-tuple-element.58.h2_in, ...), custom_call_target="tpu_custom_call" | custom-call | flops 26575110144 | bytes 41943040 | tf_op jit(solution)/shard_map/backward/pallas_call | solution.py:408
  243.5 74.4 %all-reduce = f32[16,640]{1,0:T(8,128)S(1)} all-reduce(f32[16,640]{1,0:T(8,128)S(1)} %pad_maximum_fusion.2), channel_id=2, replica_groups=mesh['section'=2,'dp'=16] {'dp'}, use_global_device_ids=true, to_apply=%region_1.2.clone | all-reduce | flops 10240 | bytes 81920
  320.1 2.4 slice.333
  322.5 4.4 collective-permute-start.4
  326.9 2.7 collective-permute-start.5
  329.6 2.8 collective-permute-start.6
  332.4 2.7 collective-permute-start.7
  335.1 3.0 collective-permute-start.8
  343.4 9.2 %readout_grads.1 = (bf16[2,512,512]{2,1,0:T(8,128)(2,1)}, bf16[2,512,512]{2,1,0:T(8,128)(2,1)}, bf16[2,512,512]{2,1,0:T(8,128)(2,1)}, bf16[2,512,512]{2,1,0:T(8,128)(2,1)}) custom-call(bf16[288,1024]{1,0:T(8,128)(2,1)} %get-tuple-element.86.y_own, bf16[288,1024]{1,0:T(8,128)(2,1)} %collective-permute-done.39.y_got, ...), custom_call_target="tpu_custom_call" | custom-call | flops 1207959552 | bytes 12582912 | tf_op jit(solution)/shard_map/readout_grads/pallas_call | solution.py:645
  369.9 4.4 fusion.4
  374.3 3.3 fusion.3
  382.9 31.1 %block_grads.2 = (bf16[4,512,512]{2,1,0:T(8,128)(2,1)}, bf16[4,512,512]{2,1,0:T(8,128)(2,1)}, bf16[4,512,512]{2,1,0:T(8,128)(2,1)}, bf16[4,512,512]{2,1,0:T(8,12...) custom-call(bf16[1152,1024]{1,0:T(8,128)(2,1)} %get-tuple-element.61.refs_0_, ...), custom_call_target="tpu_custom_call" | custom-call | flops 13287555072 | bytes 20971520 | tf_op jit(solution)/shard_map/block_grads/pallas_call | solution.py:584
  421.4 5.8 collective-permute-done.36
  431.2 45.0 %collective-permute-done.37 = bf16[3,64,512]{2,1,0:T(8,128)(2,1)S(1)} collective-permute-done((bf16[3,64,512]{2,1,0:T(8,128)(2,1)S(1)}, bf16[3,64,512]{2,1,0:T(8,128)(2,1)S(1)}, u32[]{:S(2)}, u32[]{:S(2)}) %collective-permute-start.37) | collective-permute-done | bytes 196640 | tf_op jit(solution)/shard_map/ppermute | solution.py:439
  478.7 6.6 %collective-permute-done.42 = bf16[1,2,2,128,512]{3,4,1,2,0:T(8,128)(2,1)S(1)} collective-permute-done((bf16[1,2,2,128,512]{3,4,1,2,0:T(8,128)(2,1)S(1)}, bf16[1,2,2,128,512]{3,4,1,2,0:T(8,128)(2,1)S(1)}, u32[]{:S(2)}, u32[]{:S(2)}) %collective-permute-start.42) | collective-permute-done | bytes 524320 | tf_op jit(solution)/shard_map/ppermute | solution.py:439
  486.0 5.4 collective-permute-done.46
  493.7 7.0 %collective-permute-done.43 = bf16[1,2,128,512]{2,3,1,0:T(8,128)(2,1)S(1)} collective-permute-done((bf16[1,2,128,512]{2,3,1,0:T(8,128)(2,1)S(1)}, bf16[1,2,128,512]{2,3,1,0:T(8,128)(2,1)S(1)}, u32[]{:S(2)}, u32[]{:S(2)}) %collective-permute-start.43) | collective-permute-done | bytes 262176 | tf_op jit(solution)/shard_map/ppermute | solution.py:439
  503.9 5.3 collective-permute-done.47
  513.4 6.2 collective-permute-done.28
  519.6 3.0 collective-permute-start.29
  524.0 9.6 %collective-permute-done.9 = bf16[4,2,2,2,64,512]{5,4,0,1,2,3:T(8,128)(2,1)S(1)} collective-permute-done((bf16[4,2,2,2,64,512]{5,4,0,1,2,3:T(8,128)(2,1)S(1)}, bf16[4,2,2,2,64,512]{5,4,0,1,2,3:T(8,128)(2,1)S(1)}, u32[]{:S(2)}, u32[]{:S(2)}) %collective-permute-start.9) | collective-permute-done | bytes 2097184 | tf_op jit(solution)/shard_map/ppermute | solution.py:439
  534.9 17.0 %collective-permute-done.33 = bf16[4,64,512]{2,1,0:T(8,128)(2,1)S(1)} collective-permute-done((bf16[4,64,512]{2,1,0:T(8,128)(2,1)S(1)}, bf16[4,64,512]{2,1,0:T(8,128)(2,1)S(1)}, u32[]{:S(2)}, u32[]{:S(2)}) %collective-permute-start.33) | collective-permute-done | bytes 262176 | tf_op jit(solution)/shard_map/ppermute | solution.py:439
  552.6 5.0 collective-permute-done.29
  557.6 2.8 collective-permute-start.3
  560.5 15.2 %collective-permute-done.18 = bf16[3,2,2,64,512]{4,3,0,1,2:T(8,128)(2,1)S(1)} collective-permute-done((bf16[3,2,2,64,512]{4,3,0,1,2:T(8,128)(2,1)S(1)}, bf16[3,2,2,64,512]{4,3,0,1,2:T(8,128)(2,1)S(1)}, u32[]{:S(2)}, u32[]{:S(2)}) %collective-permute-start.18) | collective-permute-done | bytes 786464 | tf_op jit(solution)/shard_map/ppermute | solution.py:439
  578.0 9.1 %collective-permute-done.19 = bf16[3,2,64,512]{3,2,0,1:T(8,128)(2,1)S(1)} collective-permute-done((bf16[3,2,64,512]{3,2,0,1:T(8,128)(2,1)S(1)}, bf16[3,2,64,512]{3,2,0,1:T(8,128)(2,1)S(1)}, u32[]{:S(2)}, u32[]{:S(2)}) %collective-permute-start.19) | collective-permute-done | bytes 393248 | tf_op jit(solution)/shard_map/ppermute | solution.py:439
  587.1 6.4 collective-permute-done.15
  594.2 6.1 collective-permute-done.20
  601.2 5.3 collective-permute-done.11
  606.8 16.7 %collective-permute-done.16 = bf16[4,64,512]{2,1,0:T(8,128)(2,1)S(1)} collective-permute-done((bf16[4,64,512]{2,1,0:T(8,128)(2,1)S(1)}, bf16[4,64,512]{2,1,0:T(8,128)(2,1)S(1)}, u32[]{:S(2)}, u32[]{:S(2)}) %collective-permute-start.16) | collective-permute-done | bytes 262176 | tf_op jit(solution)/shard_map/ppermute | solution.py:439
  623.7 7.3 %collective-permute-done.12 = bf16[4,64,512]{2,1,0:T(8,128)(2,1)S(1)} collective-permute-done((bf16[4,64,512]{2,1,0:T(8,128)(2,1)S(1)}, bf16[4,64,512]{2,1,0:T(8,128)(2,1)S(1)}, u32[]{:S(2)}, u32[]{:S(2)}) %collective-permute-start.12) | collective-permute-done | bytes 262176 | tf_op jit(solution)/shard_map/ppermute | solution.py:439
  634.4 2.4 reshape.566
  642.7 2.4 fusion
  646.1 3.5 copy.96
  649.6 4.5 reshape.580
  (229 shorter events, 101.3 us)
Async XLA Ops:
  51.5 8.9 %collective-permute-start = (bf16[288,1024]{1,0:T(8,128)(2,1)}, bf16[288,1024]{1,0:T(8,128)(2,1)}, u32[]{:S(2)}, u32[]{:S(2)}) collective-permute-start(bf16[288,1024]{1,0:T(8,128)(2,1)} %get-tuple-element.50), channel_id=1, source_target_pairs={{0,16},{1,17},{2,18},{3,19},{4,20},{5,21},{6,22},{7,23},{8,24},{9,... | collective-permute-start | bytes 1769480 | tf_op jit(solution)/shard_map/ppermute | solution.py:668
  81.4 19.0 %collective-permute-start.21 = (bf16[288,1024]{1,0:T(8,128)(2,1)}, bf16[288,1024]{1,0:T(8,128)(2,1)S(1)}, u32[]{:S(2)}, u32[]{:S(2)}) collective-permute-start(bf16[288,1024]{1,0:T(8,128)(2,1)} %get-tuple-element.72.refs_0_), channel_id=1, source_target_pairs={{16,0},{17,1},{18,2},{19,3},{20,4},{21,5},{22,6},{23,7},{24,8},{25... | collective-permute-start | bytes 1769480 | tf_op jit(solution)/shard_map/ppermute | solution.py:668
  82.7 17.7 %collective-permute-start.22 = (bf16[288,1024]{1,0:T(8,128)(2,1)}, bf16[288,1024]{1,0:T(8,128)(2,1)S(1)}, u32[]{:S(2)}, u32[]{:S(2)}) collective-permute-start(bf16[288,1024]{1,0:T(8,128)(2,1)} %get-tuple-element.73.refs_1_), channel_id=1, source_target_pairs={{16,0},{17,1},{18,2},{19,3},{20,4},{21,5},{22,6},{23,7},{24,8},{25... | collective-permute-start | bytes 1769480 | tf_op jit(solution)/shard_map/ppermute | solution.py:668
  95.6 22.2 %collective-permute-start.23 = (bf16[288,1024]{1,0:T(8,128)(2,1)}, bf16[288,1024]{1,0:T(8,128)(2,1)S(1)}, u32[]{:S(2)}, u32[]{:S(2)}) collective-permute-start(bf16[288,1024]{1,0:T(8,128)(2,1)} %get-tuple-element.74.refs_2_), channel_id=1, source_target_pairs={{16,0},{17,1},{18,2},{19,3},{20,4},{21,5},{22,6},{23,7},{24,8},{25... | collective-permute-start | bytes 1769480 | tf_op jit(solution)/shard_map/ppermute | solution.py:668
  96.9 22.2 %collective-permute-start.24 = (bf16[288,1024]{1,0:T(8,128)(2,1)}, bf16[288,1024]{1,0:T(8,128)(2,1)S(1)}, u32[]{:S(2)}, u32[]{:S(2)}) collective-permute-start(bf16[288,1024]{1,0:T(8,128)(2,1)} %get-tuple-element.75.refs_3_), channel_id=1, source_target_pairs={{16,0},{17,1},{18,2},{19,3},{20,4},{21,5},{22,6},{23,7},{24,8},{25... | collective-permute-start | bytes 1769480 | tf_op jit(solution)/shard_map/ppermute | solution.py:668
  98.2 22.2 %collective-permute-start.25 = (bf16[288,1024]{1,0:T(8,128)(2,1)}, bf16[288,1024]{1,0:T(8,128)(2,1)S(1)}, u32[]{:S(2)}, u32[]{:S(2)}) collective-permute-start(bf16[288,1024]{1,0:T(8,128)(2,1)} %get-tuple-element.76.refs_4_), channel_id=1, source_target_pairs={{16,0},{17,1},{18,2},{19,3},{20,4},{21,5},{22,6},{23,7},{24,8},{25... | collective-permute-start | bytes 1769480 | tf_op jit(solution)/shard_map/ppermute | solution.py:668
  142.0 37.5 %collective-permute-start.34 = (bf16[3,2,2,2,64,512]{5,4,0,2,3,1:T(8,128)(2,1)}, bf16[3,2,2,2,64,512]{5,4,0,2,3,1:T(8,128)(2,1)}, u32[]{:S(2)}, u32[]{:S(2)}) collective-permute-start(bf16[3,2,2,2,64,512]{5,4,0,2,3,1:T(8,128)(2,1)} %copy.93), channel_id=1, source_target_pairs={{0,4},{1,5},{2,6},{3,7},{4,0},{5,1},{6,2},{7,3},{8,12},{9,13},{10,... | collective-permute-start | bytes 4718600 | tf_op jit(solution)/shard_map/ppermute | solution.py:439
  145.6 39.0 %collective-permute-start.2 = (bf16[288,1024]{1,0:T(8,128)(2,1)}, bf16[288,1024]{1,0:T(8,128)(2,1)S(1)}, u32[]{:S(2)}, u32[]{:S(2)}) collective-permute-start(bf16[288,1024]{1,0:T(8,128)(2,1)} %get-tuple-element.56), channel_id=1, source_target_pairs={{16,0},{17,1},{18,2},{19,3},{20,4},{21,5},{22,6},{23,7},{24,8},{25... | collective-permute-start | bytes 1769480 | tf_op jit(solution)/shard_map/ppermute | solution.py:668
  146.9 171.9 %collective-permute-start.39 = (bf16[288,1024]{1,0:T(8,128)(2,1)}, bf16[288,1024]{1,0:T(8,128)(2,1)}, u32[]{:S(2)}, u32[]{:S(2)}) collective-permute-start(bf16[288,1024]{1,0:T(8,128)(2,1)} %get-tuple-element.86.y_own), channel_id=1, source_target_pairs={{16,0},{17,1},{18,2},{19,3},{20,4},{21,5},{22,6},{23,7},{24,8},{25... | collective-permute-start | bytes 1769480 | tf_op jit(solution)/shard_map/ppermute | solution.py:668
  148.2 178.7 %collective-permute-start.40 = (bf16[288,4096]{1,0:T(8,128)(2,1)}, bf16[288,4096]{1,0:T(8,128)(2,1)}, u32[]{:S(2)}, u32[]{:S(2)}) collective-permute-start(bf16[288,4096]{1,0:T(8,128)(2,1)} %get-tuple-element.87.d_own), channel_id=1, source_target_pairs={{16,0},{17,1},{18,2},{19,3},{20,4},{21,5},{22,6},{23,7},{24,8},{25... | collective-permute-start | bytes 7077896 | tf_op jit(solution)/shard_map/ppermute | solution.py:668
  151.2 178.4 %collective-permute-start.30 = (bf16[4,2,2,2,64,512]{5,4,0,1,2,3:T(8,128)(2,1)}, bf16[4,2,2,2,64,512]{5,4,0,1,2,3:T(8,128)(2,1)}, u32[]{:S(2)}, u32[]{:S(2)}) collective-permute-start(bf16[4,2,2,2,64,512]{5,4,0,1,2,3:T(8,128)(2,1)} %copy.90), channel_id=1, source_target_pairs={{0,2},{1,3},{2,0},{3,1},{4,6},{5,7},{6,4},{7,5},{8,10},{9,11},{10,... | collective-permute-start | bytes 6291464 | tf_op jit(solution)/shard_map/ppermute | solution.py:439
  179.5 152.9 %collective-permute-start.26 = (bf16[4,2,2,2,64,512]{5,4,0,1,2,3:T(8,128)(2,1)}, bf16[4,2,2,2,64,512]{5,4,0,1,2,3:T(8,128)(2,1)}, u32[]{:S(2)}, u32[]{:S(2)}) collective-permute-start(bf16[4,2,2,2,64,512]{5,4,0,1,2,3:T(8,128)(2,1)} %copy.87), channel_id=1, source_target_pairs={{0,1},{1,0},{2,3},{3,2},{4,5},{5,4},{6,7},{7,6},{8,9},{9,8},{10,11... | collective-permute-start | bytes 6291464 | tf_op jit(solution)/shard_map/ppermute | solution.py:439
  184.6 150.6 %collective-permute-start.35 = (bf16[3,2,2,64,512]{4,3,0,1,2:T(8,128)(2,1)}, bf16[3,2,2,64,512]{4,3,0,1,2:T(8,128)(2,1)S(1)}, u32[]{:S(2)}, u32[]{:S(2)}) collective-permute-start(bf16[3,2,2,64,512]{4,3,0,1,2:T(8,128)(2,1)} %get-tuple-element.150), channel_id=1, source_target_pairs={{0,8},{1,9},{2,10},{3,11},{4,12},{5,13},{6,14},{7,15},{8,0},{9,1},... | collective-permute-start | bytes 2359304 | tf_op jit(solution)/shard_map/ppermute | solution.py:439
  322.5 56.3 %collective-permute-start.4 = (bf16[1152,1024]{1,0:T(8,128)(2,1)}, bf16[1152,1024]{1,0:T(8,128)(2,1)}, u32[]{:S(2)}, u32[]{:S(2)}) collective-permute-start(bf16[1152,1024]{1,0:T(8,128)(2,1)} %get-tuple-element.61.refs_0_), channel_id=1, source_target_pairs={{0,16},{1,17},{2,18},{3,19},{4,20},{5,21},{6,22},{7,23},{8,24},{9,... | collective-permute-start | bytes 7077896 | tf_op jit(solution)/shard_map/ppermute | solution.py:668
  326.9 51.9 %collective-permute-start.5 = (bf16[1152,1024]{1,0:T(8,128)(2,1)}, bf16[1152,1024]{1,0:T(8,128)(2,1)}, u32[]{:S(2)}, u32[]{:S(2)}) collective-permute-start(bf16[1152,1024]{1,0:T(8,128)(2,1)} %get-tuple-element.62.refs_1_), channel_id=1, source_target_pairs={{0,16},{1,17},{2,18},{3,19},{4,20},{5,21},{6,22},{7,23},{8,24},{9,... | collective-permute-start | bytes 7077896 | tf_op jit(solution)/shard_map/ppermute | solution.py:668
  329.6 49.3 %collective-permute-start.6 = (bf16[1152,1024]{1,0:T(8,128)(2,1)}, bf16[1152,1024]{1,0:T(8,128)(2,1)}, u32[]{:S(2)}, u32[]{:S(2)}) collective-permute-start(bf16[1152,1024]{1,0:T(8,128)(2,1)} %get-tuple-element.63.refs_2_), channel_id=1, source_target_pairs={{0,16},{1,17},{2,18},{3,19},{4,20},{5,21},{6,22},{7,23},{8,24},{9,... | collective-permute-start | bytes 7077896 | tf_op jit(solution)/shard_map/ppermute | solution.py:668
  332.4 48.5 %collective-permute-start.7 = (bf16[1152,1024]{1,0:T(8,128)(2,1)}, bf16[1152,1024]{1,0:T(8,128)(2,1)}, u32[]{:S(2)}, u32[]{:S(2)}) collective-permute-start(bf16[1152,1024]{1,0:T(8,128)(2,1)} %get-tuple-element.64.refs_3_), channel_id=1, source_target_pairs={{0,16},{1,17},{2,18},{3,19},{4,20},{5,21},{6,22},{7,23},{8,24},{9,... | collective-permute-start | bytes 7077896 | tf_op jit(solution)/shard_map/ppermute | solution.py:668
  335.1 47.7 %collective-permute-start.8 = (bf16[1152,1024]{1,0:T(8,128)(2,1)}, bf16[1152,1024]{1,0:T(8,128)(2,1)}, u32[]{:S(2)}, u32[]{:S(2)}) collective-permute-start(bf16[1152,1024]{1,0:T(8,128)(2,1)} %get-tuple-element.65.refs_4_), channel_id=1, source_target_pairs={{0,16},{1,17},{2,18},{3,19},{4,20},{5,21},{6,22},{7,23},{8,24},{9,... | collective-permute-start | bytes 7077896 | tf_op jit(solution)/shard_map/ppermute | solution.py:668
  378.8 48.5 %collective-permute-start.41 = (bf16[1,2,2,2,128,512]{4,5,1,2,3,0:T(8,128)(2,1)}, bf16[1,2,2,2,128,512]{4,5,1,2,3,0:T(8,128)(2,1)}, u32[]{:S(2)}, u32[]{:S(2)}) collective-permute-start(bf16[1,2,2,2,128,512]{4,5,1,2,3,0:T(8,128)(2,1)} %copy.97), channel_id=1, source_target_pairs={{0,1},{1,0},{2,3},{3,2},{4,5},{5,4},{6,7},{7,6},{8,9},{9,8},{10,11... | collective-permute-start | bytes 3145736 | tf_op jit(solution)/shard_map/ppermute | solution.py:439
  378.8 50.1 %collective-permute-start.45 = (bf16[1,2,2,2,128,512]{4,5,1,2,3,0:T(8,128)(2,1)}, bf16[1,2,2,2,128,512]{4,5,1,2,3,0:T(8,128)(2,1)S(1)}, u32[]{:S(2)}, u32[]{:S(2)}) collective-permute-start(bf16[1,2,2,2,128,512]{4,5,1,2,3,0:T(8,128)(2,1)} %copy.100), channel_id=1, source_target_pairs={{0,2},{1,3},{2,0},{3,1},{4,6},{5,7},{6,4},{7,5},{8,10},{9,11},{10,... | collective-permute-start | bytes 3145736 | tf_op jit(solution)/shard_map/ppermute | solution.py:439
  378.9 97.6 %collective-permute-start.31 = (bf16[4,2,2,64,512]{4,3,0,1,2:T(8,128)(2,1)}, bf16[4,2,2,64,512]{4,3,0,1,2:T(8,128)(2,1)}, u32[]{:S(2)}, u32[]{:S(2)}) collective-permute-start(bf16[4,2,2,64,512]{4,3,0,1,2:T(8,128)(2,1)} %get-tuple-element.136), channel_id=1, source_target_pairs={{0,1},{1,0},{2,3},{3,2},{4,5},{5,4},{6,7},{7,6},{8,9},{9,8},{10,11... | collective-permute-start | bytes 3145736 | tf_op jit(solution)/shard_map/ppermute | solution.py:439
  380.9 112.4 %collective-permute-start.27 = (bf16[4,2,2,64,512]{4,3,0,1,2:T(8,128)(2,1)}, bf16[4,2,2,64,512]{4,3,0,1,2:T(8,128)(2,1)}, u32[]{:S(2)}, u32[]{:S(2)}) collective-permute-start(bf16[4,2,2,64,512]{4,3,0,1,2:T(8,128)(2,1)} %get-tuple-element.132), channel_id=1, source_target_pairs={{0,2},{1,3},{2,0},{3,1},{4,6},{5,7},{6,4},{7,5},{8,10},{9,11},{10,... | collective-permute-start | bytes 3145736 | tf_op jit(solution)/shard_map/ppermute | solution.py:439
  382.9 44.3 %collective-permute-start.36 = (bf16[3,2,64,512]{3,2,0,1:T(8,128)(2,1)S(1)}, bf16[3,2,64,512]{3,2,0,1:T(8,128)(2,1)S(1)}, u32[]{:S(2)}, u32[]{:S(2)}) collective-permute-start(bf16[3,2,64,512]{3,2,0,1:T(8,128)(2,1)S(1)} %get-tuple-element.122), channel_id=1, source_target_pairs={{0,1},{1,0},{2,3},{3,2},{4,5},{5,4},{6,7},{7,6},{8,9},{9,8},{10,11... | collective-permute-start | bytes 1179656 | tf_op jit(solution)/shard_map/ppermute | solution.py:439
  427.2 92.4 %collective-permute-start.17 = (bf16[3,2,2,2,64,512]{5,4,0,2,3,1:T(8,128)(2,1)S(1)}, bf16[3,2,2,2,64,512]{5,4,0,2,3,1:T(8,128)(2,1)S(1)}, u32[]{:S(2)}, u32[]{:S(2)}) collective-permute-start(bf16[3,2,2,2,64,512]{5,4,0,2,3,1:T(8,128)(2,1)S(1)} %copy.84), channel_id=1, source_target_pairs={{0,4},{1,5},{2,6},{3,7},{4,0},{5,1},{6,2},{7,3},{8,12},{9,13},{10,... | collective-permute-start | bytes 4718600 | tf_op jit(solution)/shard_map/ppermute | solution.py:439
  427.3 95.9 %collective-permute-start.13 = (bf16[4,2,2,2,64,512]{5,4,0,1,2,3:T(8,128)(2,1)S(1)}, bf16[4,2,2,2,64,512]{5,4,0,1,2,3:T(8,128)(2,1)S(1)}, u32[]{:S(2)}, u32[]{:S(2)}) collective-permute-start(bf16[4,2,2,2,64,512]{5,4,0,1,2,3:T(8,128)(2,1)S(1)} %copy.81), channel_id=1, source_target_pairs={{0,2},{1,3},{2,0},{3,1},{4,6},{5,7},{6,4},{7,5},{8,10},{9,11},{10,... | collective-permute-start | bytes 6291464 | tf_op jit(solution)/shard_map/ppermute | solution.py:439
  428.9 47.2 %collective-permute-start.37 = (bf16[3,64,512]{2,1,0:T(8,128)(2,1)S(1)}, bf16[3,64,512]{2,1,0:T(8,128)(2,1)S(1)}, u32[]{:S(2)}, u32[]{:S(2)}) collective-permute-start(bf16[3,64,512]{2,1,0:T(8,128)(2,1)S(1)} %fusion.66), channel_id=1, source_target_pairs={{0,2},{1,3},{2,0},{3,1},{4,6},{5,7},{6,4},{7,5},{8,10},{9,11},{10,... | collective-permute-start | bytes 589832 | tf_op jit(solution)/shard_map/ppermute | solution.py:439
  476.1 9.2 %collective-permute-start.42 = (bf16[1,2,2,128,512]{3,4,1,2,0:T(8,128)(2,1)S(1)}, bf16[1,2,2,128,512]{3,4,1,2,0:T(8,128)(2,1)S(1)}, u32[]{:S(2)}, u32[]{:S(2)}) collective-permute-start(bf16[1,2,2,128,512]{3,4,1,2,0:T(8,128)(2,1)S(1)} %get-tuple-element.158), channel_id=1, source_target_pairs={{0,2},{1,3},{2,0},{3,1},{4,6},{5,7},{6,4},{7,5},{8,10},{9,11},{10,... | collective-permute-start | bytes 1572872 | tf_op jit(solution)/shard_map/ppermute | solution.py:439
  476.5 14.9 %collective-permute-start.46 = (bf16[1,2,2,128,512]{3,4,1,2,0:T(8,128)(2,1)S(1)}, bf16[1,2,2,128,512]{3,4,1,2,0:T(8,128)(2,1)S(1)}, u32[]{:S(2)}, u32[]{:S(2)}) collective-permute-start(bf16[1,2,2,128,512]{3,4,1,2,0:T(8,128)(2,1)S(1)} %get-tuple-element.154), channel_id=1, source_target_pairs={{0,1},{1,0},{2,3},{3,2},{4,5},{5,4},{6,7},{7,6},{8,9},{9,8},{10,11... | collective-permute-start | bytes 1572872 | tf_op jit(solution)/shard_map/ppermute | solution.py:439
  485.3 48.3 %collective-permute-start.9 = (bf16[4,2,2,2,64,512]{5,4,0,1,2,3:T(8,128)(2,1)S(1)}, bf16[4,2,2,2,64,512]{5,4,0,1,2,3:T(8,128)(2,1)S(1)}, u32[]{:S(2)}, u32[]{:S(2)}) collective-permute-start(bf16[4,2,2,2,64,512]{5,4,0,1,2,3:T(8,128)(2,1)S(1)} %copy.78), channel_id=1, source_target_pairs={{0,1},{1,0},{2,3},{3,2},{4,5},{5,4},{6,7},{7,6},{8,9},{9,8},{10,11... | collective-permute-start | bytes 6291464 | tf_op jit(solution)/shard_map/ppermute | solution.py:439
  491.4 9.2 %collective-permute-start.43 = (bf16[1,2,128,512]{2,3,1,0:T(8,128)(2,1)S(1)}, bf16[1,2,128,512]{2,3,1,0:T(8,128)(2,1)S(1)}, u32[]{:S(2)}, u32[]{:S(2)}) collective-permute-start(bf16[1,2,128,512]{2,3,1,0:T(8,128)(2,1)S(1)} %get-tuple-element.144), channel_id=1, source_target_pairs={{0,4},{1,5},{2,6},{3,7},{4,0},{5,1},{6,2},{7,3},{8,12},{9,13},{10,... | collective-permute-start | bytes 786440 | tf_op jit(solution)/shard_map/ppermute | solution.py:439
  493.3 18.7 %collective-permute-start.32 = (bf16[4,2,64,512]{3,2,0,1:T(8,128)(2,1)S(1)}, bf16[4,2,64,512]{3,2,0,1:T(8,128)(2,1)S(1)}, u32[]{:S(2)}, u32[]{:S(2)}) collective-permute-start(bf16[4,2,64,512]{3,2,0,1:T(8,128)(2,1)S(1)} %get-tuple-element.114), channel_id=1, source_target_pairs={{0,4},{1,5},{2,6},{3,7},{4,0},{5,1},{6,2},{7,3},{8,12},{9,13},{10,... | collective-permute-start | bytes 1572872 | tf_op jit(solution)/shard_map/ppermute | solution.py:439
  500.7 8.5 %collective-permute-start.47 = (bf16[1,2,128,512]{2,3,1,0:T(8,128)(2,1)S(1)}, bf16[1,2,128,512]{2,3,1,0:T(8,128)(2,1)S(1)}, u32[]{:S(2)}, u32[]{:S(2)}) collective-permute-start(bf16[1,2,128,512]{2,3,1,0:T(8,128)(2,1)S(1)} %get-tuple-element.142), channel_id=1, source_target_pairs={{0,4},{1,5},{2,6},{3,7},{4,0},{5,1},{6,2},{7,3},{8,12},{9,13},{10,... | collective-permute-start | bytes 786440 | tf_op jit(solution)/shard_map/ppermute | solution.py:439
  509.2 10.4 %collective-permute-start.28 = (bf16[4,2,64,512]{3,2,0,1:T(8,128)(2,1)S(1)}, bf16[4,2,64,512]{3,2,0,1:T(8,128)(2,1)S(1)}, u32[]{:S(2)}, u32[]{:S(2)}) collective-permute-start(bf16[4,2,64,512]{3,2,0,1:T(8,128)(2,1)S(1)} %get-tuple-element.112), channel_id=1, source_target_pairs={{0,4},{1,5},{2,6},{3,7},{4,0},{5,1},{6,2},{7,3},{8,12},{9,13},{10,... | collective-permute-start | bytes 1572872 | tf_op jit(solution)/shard_map/ppermute | solution.py:439
  512.0 120.5 %collective-permute-start.1 = (bf16[288,2048]{1,0:T(8,128)(2,1)S(1)}, bf16[288,2048]{1,0:T(8,128)(2,1)S(1)}, u32[]{:S(2)}, u32[]{:S(2)}) collective-permute-start(bf16[288,2048]{1,0:T(8,128)(2,1)S(1)} %copy-done.23), channel_id=1, source_target_pairs={{16,0},{17,1},{18,2},{19,3},{20,4},{21,5},{22,6},{23,7},{24,8},{25... | collective-permute-start | bytes 3538952 | tf_op jit(solution)/shard_map/ppermute | solution.py:668
  519.5 32.4 %collective-permute-start.33 = (bf16[4,64,512]{2,1,0:T(8,128)(2,1)S(1)}, bf16[4,64,512]{2,1,0:T(8,128)(2,1)S(1)}, u32[]{:S(2)}, u32[]{:S(2)}) collective-permute-start(bf16[4,64,512]{2,1,0:T(8,128)(2,1)S(1)} %fusion.56), channel_id=1, source_target_pairs={{0,8},{1,9},{2,10},{3,11},{4,12},{5,13},{6,14},{7,15},{8,0},{9,1},... | collective-permute-start | bytes 786440 | tf_op jit(solution)/shard_map/ppermute | solution.py:439
  519.6 37.9 %collective-permute-start.29 = (bf16[4,64,512]{2,1,0:T(8,128)(2,1)S(1)}, bf16[4,64,512]{2,1,0:T(8,128)(2,1)S(1)}, u32[]{:S(2)}, u32[]{:S(2)}) collective-permute-start(bf16[4,64,512]{2,1,0:T(8,128)(2,1)S(1)} %fusion.55), channel_id=1, source_target_pairs={{0,8},{1,9},{2,10},{3,11},{4,12},{5,13},{6,14},{7,15},{8,0},{9,1},... | collective-permute-start | bytes 786440 | tf_op jit(solution)/shard_map/ppermute | solution.py:439
  523.2 52.6 %collective-permute-start.18 = (bf16[3,2,2,64,512]{4,3,0,1,2:T(8,128)(2,1)S(1)}, bf16[3,2,2,64,512]{4,3,0,1,2:T(8,128)(2,1)S(1)}, u32[]{:S(2)}, u32[]{:S(2)}) collective-permute-start(bf16[3,2,2,64,512]{4,3,0,1,2:T(8,128)(2,1)S(1)} %get-tuple-element.146), channel_id=1, source_target_pairs={{0,8},{1,9},{2,10},{3,11},{4,12},{5,13},{6,14},{7,15},{8,0},{9,1},... | collective-permute-start | bytes 2359304 | tf_op jit(solution)/shard_map/ppermute | solution.py:439
  533.6 42.4 %collective-permute-start.14 = (bf16[4,2,2,64,512]{4,3,0,1,2:T(8,128)(2,1)S(1)}, bf16[4,2,2,64,512]{4,3,0,1,2:T(8,128)(2,1)S(1)}, u32[]{:S(2)}, u32[]{:S(2)}) collective-permute-start(bf16[4,2,2,64,512]{4,3,0,1,2:T(8,128)(2,1)S(1)} %get-tuple-element.128), channel_id=1, source_target_pairs={{0,1},{1,0},{2,3},{3,2},{4,5},{5,4},{6,7},{7,6},{8,9},{9,8},{10,11... | collective-permute-start | bytes 3145736 | tf_op jit(solution)/shard_map/ppermute | solution.py:439
  551.9 25.6 %collective-permute-start.10 = (bf16[4,2,2,64,512]{4,3,0,1,2:T(8,128)(2,1)S(1)}, bf16[4,2,2,64,512]{4,3,0,1,2:T(8,128)(2,1)S(1)}, u32[]{:S(2)}, u32[]{:S(2)}) collective-permute-start(bf16[4,2,2,64,512]{4,3,0,1,2:T(8,128)(2,1)S(1)} %get-tuple-element.124), channel_id=1, source_target_pairs={{0,2},{1,3},{2,0},{3,1},{4,6},{5,7},{6,4},{7,5},{8,10},{9,11},{10,... | collective-permute-start | bytes 3145736 | tf_op jit(solution)/shard_map/ppermute | solution.py:439
  557.6 82.7 %collective-permute-start.3 = (bf16[1152,512]{1,0:T(8,128)(2,1)}, bf16[1152,512]{1,0:T(8,128)(2,1)}, u32[]{:S(2)}, u32[]{:S(2)}) collective-permute-start(bf16[1152,512]{1,0:T(8,128)(2,1)} %slice.336), channel_id=1, source_target_pairs={{0,16},{1,17},{2,18},{3,19},{4,20},{5,21},{6,22},{7,23},{8,24},{9,... | collective-permute-start | bytes 3538952 | tf_op jit(solution)/shard_map/ppermute | solution.py:668
  575.7 63.4 %collective-permute-start.44 = (bf16[1,128,512]{1,2,0:T(8,128)(2,1)}, bf16[1,128,512]{1,2,0:T(8,128)(2,1)}, u32[]{:S(2)}, u32[]{:S(2)}) collective-permute-start(bf16[1,128,512]{1,2,0:T(8,128)(2,1)} %fusion.67), channel_id=1, source_target_pairs={{0,8},{1,9},{2,10},{3,11},{4,12},{5,13},{6,14},{7,15},{8,0},{9,1},... | collective-permute-start | bytes 393224 | tf_op jit(solution)/shard_map/ppermute | solution.py:439
  576.0 11.1 %collective-permute-start.19 = (bf16[3,2,64,512]{3,2,0,1:T(8,128)(2,1)S(1)}, bf16[3,2,64,512]{3,2,0,1:T(8,128)(2,1)S(1)}, u32[]{:S(2)}, u32[]{:S(2)}) collective-permute-start(bf16[3,2,64,512]{3,2,0,1:T(8,128)(2,1)S(1)} %get-tuple-element.120), channel_id=1, source_target_pairs={{0,1},{1,0},{2,3},{3,2},{4,5},{5,4},{6,7},{7,6},{8,9},{9,8},{10,11... | collective-permute-start | bytes 1179656 | tf_op jit(solution)/shard_map/ppermute | solution.py:439
  577.6 16.0 %collective-permute-start.15 = (bf16[4,2,64,512]{3,2,0,1:T(8,128)(2,1)S(1)}, bf16[4,2,64,512]{3,2,0,1:T(8,128)(2,1)S(1)}, u32[]{:S(2)}, u32[]{:S(2)}) collective-permute-start(bf16[4,2,64,512]{3,2,0,1:T(8,128)(2,1)S(1)} %get-tuple-element.110), channel_id=1, source_target_pairs={{0,4},{1,5},{2,6},{3,7},{4,0},{5,1},{6,2},{7,3},{8,12},{9,13},{10,... | collective-permute-start | bytes 1572872 | tf_op jit(solution)/shard_map/ppermute | solution.py:439
  587.1 19.4 %collective-permute-start.11 = (bf16[4,2,64,512]{3,2,0,1:T(8,128)(2,1)S(1)}, bf16[4,2,64,512]{3,2,0,1:T(8,128)(2,1)S(1)}, u32[]{:S(2)}, u32[]{:S(2)}) collective-permute-start(bf16[4,2,64,512]{3,2,0,1:T(8,128)(2,1)S(1)} %get-tuple-element.108), channel_id=1, source_target_pairs={{0,4},{1,5},{2,6},{3,7},{4,0},{5,1},{6,2},{7,3},{8,12},{9,13},{10,... | collective-permute-start | bytes 1572872 | tf_op jit(solution)/shard_map/ppermute | solution.py:439
  600.3 23.3 %collective-permute-start.16 = (bf16[4,64,512]{2,1,0:T(8,128)(2,1)S(1)}, bf16[4,64,512]{2,1,0:T(8,128)(2,1)S(1)}, u32[]{:S(2)}, u32[]{:S(2)}) collective-permute-start(bf16[4,64,512]{2,1,0:T(8,128)(2,1)S(1)} %fusion.54), channel_id=1, source_target_pairs={{0,8},{1,9},{2,10},{3,11},{4,12},{5,13},{6,14},{7,15},{8,0},{9,1},... | collective-permute-start | bytes 786440 | tf_op jit(solution)/shard_map/ppermute | solution.py:439
  606.5 32.7 %collective-permute-start.48 = (bf16[1,128,512]{1,2,0:T(8,128)(2,1)}, bf16[1,128,512]{1,2,0:T(8,128)(2,1)}, u32[]{:S(2)}, u32[]{:S(2)}) collective-permute-start(bf16[1,128,512]{1,2,0:T(8,128)(2,1)} %fusion.68), channel_id=1, source_target_pairs={{0,8},{1,9},{2,10},{3,11},{4,12},{5,13},{6,14},{7,15},{8,0},{9,1},... | collective-permute-start | bytes 393224 | tf_op jit(solution)/shard_map/ppermute | solution.py:439
  623.6 7.4 %collective-permute-start.12 = (bf16[4,64,512]{2,1,0:T(8,128)(2,1)S(1)}, bf16[4,64,512]{2,1,0:T(8,128)(2,1)S(1)}, u32[]{:S(2)}, u32[]{:S(2)}) collective-permute-start(bf16[4,64,512]{2,1,0:T(8,128)(2,1)S(1)} %fusion.53), channel_id=1, source_target_pairs={{0,8},{1,9},{2,10},{3,11},{4,12},{5,13},{6,14},{7,15},{8,0},{9,1},... | collective-permute-start | bytes 786440 | tf_op jit(solution)/shard_map/ppermute | solution.py:439
  632.5 10.2 %collective-permute-start.38 = (f32[11,64,512]{2,1,0:T(8,128)}, f32[11,64,512]{2,1,0:T(8,128)}, u32[]{:S(2)}, u32[]{:S(2)}) collective-permute-start(f32[11,64,512]{2,1,0:T(8,128)} %get-tuple-element.119), channel_id=1, source_target_pairs={{0,16},{16,0},{1,17},{17,1},{2,18},{18,2},{3,19},{19,3},{4,20},{20... | collective-permute-start | bytes 4325384 | tf_op jit(solution)/shard_map/ppermute | solution.py:672
  (45 other events, 357.2 us)
